TPU v7x, 256 devices: a whole 4x4x8 slice. The times are simulated.
256 devices in a mesh: prow: 32 (over x, z), pcol: 8 (over y, core).
Axes of the slice: x: 4, y: 4, z: 8, core: 2. Of those that a mesh axis runs over, the one named last changes fastest.
Arguments:
- matrix: float32 [2, 8192, 8, 2048], P(None, 'prow', None, 'pcol'), may hold values from -6 to 6
- pattern: int32 [64, 64], replicated, may hold values from 0 to 1, as said below
- row_perm: int32 [2, 8192], P(None, 'prow'), may hold values from 0 to 255, as said below
- lower_inv: float32 [3, 256, 256], replicated, as said below
- upper_inv: float32 [3, 256, 256], replicated, as said below
Outputs:
- factored: float32 [2, 8192, 8, 2048], P(None, 'prow', None, 'pcol')
Inputs may be any that keep to these rules, and one draw needn't show every extreme that they name: `pattern`: 1 where a block is kept, 0 where it is dropped; every diagonal entry is 1. `row_perm`: each aligned group of 256 entries is a permutation of 0 to 255, the source row within the same block row. `lower_inv`: lower triangular with ones on the diagonal. `upper_inv`: upper triangular with nonzero diagonal.
All inputs are finite; a program needn't handle non-finite values.
Results may differ from a plain program's by a relative error of at most 0.0001.
Values sent between devices are 32-bit elements; how exact they have to be, the bound alone decides.
No kernel may reach another device: no remote copies, remote signals or barrier semaphores. Data moves between devices by JAX's collectives and lax.ppermute only.
A program may use at most 64 MiB of HBM per device.

v0:
```python
import jax
import jax.numpy as jnp
from jax import lax
from jax.sharding import PartitionSpec as P

PANELS = 3


def broadcast(array, axis, root):
    mine = lax.axis_index(axis) == root
    return lax.psum(jnp.where(mine, array, jnp.zeros_like(array)), axis)


def on_device(matrix, pattern, row_perm, lower_inv, upper_inv):
    high = lax.Precision.HIGHEST
    row_count = lax.axis_size("prow")
    col_count = lax.axis_size("pcol")
    row_here = lax.axis_index("prow")
    col_here = lax.axis_index("pcol")
    row_blocks = matrix.shape[0]
    col_blocks = matrix.shape[2]
    nblocks = pattern.shape[0]
    row_ids = jnp.arange(row_blocks, dtype=jnp.int32) * row_count + row_here
    col_ids = jnp.arange(col_blocks, dtype=jnp.int32) * col_count + col_here
    every = jnp.arange(nblocks, dtype=jnp.int32)
    row_select = (row_ids[:, None] == every[None, :]).astype(jnp.float32)
    col_select = (col_ids[:, None] == every[None, :]).astype(jnp.float32)
    local_mask = jnp.dot(
        jnp.dot(row_select, pattern.astype(jnp.float32), precision=high),
        col_select.T,
        precision=high,
    )
    blocks = jax.vmap(lambda single, rows: single[rows])(matrix, row_perm)
    blocks = blocks * local_mask[:, None, :, None]

    def panels(column, block_row, step):
        lpanel = jnp.einsum("irt,ts->irs", column, upper_inv[step], precision=high)
        left_block = broadcast(lpanel, "pcol", step % col_count)
        upanel = jnp.einsum("rt,tjs->rjs", lower_inv[step], block_row, precision=high)
        upper_block = broadcast(upanel, "prow", step % row_count)
        return (left_block, upper_block)

    left_block, upper_block = panels(blocks[:, :, 0, :], blocks[0], 0)
    for step in range(PANELS):
        live_rows = row_ids > step
        live_cols = col_ids > step
        weight = (
            local_mask
            * live_rows[:, None].astype(jnp.float32)
            * live_cols[None, :].astype(jnp.float32)
        )
        after = step + 1
        coming = (left_block, upper_block)
        update = jnp.einsum("irt,tjs->irjs", left_block, upper_block, precision=high)
        blocks = blocks - weight[:, None, :, None] * update
        own_col = step // col_count
        own_row = step // row_count
        keep_col = jnp.logical_and(col_here == step % col_count, live_rows)[:, None, None]
        blocks = blocks.at[:, :, own_col, :].set(
            jnp.where(keep_col, left_block, blocks[:, :, own_col, :])
        )
        keep_row = jnp.logical_and(row_here == step % row_count, live_cols)[None, :, None]
        blocks = blocks.at[own_row].set(jnp.where(keep_row, upper_block, blocks[own_row]))
        if after < PANELS:
            coming = panels(blocks[:, :, after // col_count, :], blocks[after // row_count], after)
            left_block, upper_block = coming
    return blocks


def solution(mesh):
    in_specs = (P(None, "prow", None, "pcol"), P(), P(None, "prow"), P(), P())
    out_specs = P(None, "prow", None, "pcol")
    return jax.shard_map(
        on_device, mesh=mesh, in_specs=in_specs, out_specs=out_specs, check_vma=False
    )
```

profile of v0, /device:TPU:1, one launch (start us, length us, event | category | flops | bytes accessed | tf_op | source)
XLA Modules:
  0.0 733.2 jit_solution(11967416934911036885)
XLA Ops:
  6.6 0.9 fusion.33
  7.8 0.7 fusion.40
  8.5 8.1 %gather_fusion = f32[512,8,256]{2,1,0:T(8,128)} fusion(f32[2,256,8,256]{3,2,1,0:T(8,128)} %param.17, s32[512]{0:T(512)S(1)} %bitcast.152), kind=kCustom, calls=%fused_computation | custom fusion | bytes 8392704 | tf_op jit(solution)/shard_map/vmap()/gather | solution.py:33
  16.6 5.5 copy.6
  22.1 2.8 broadcast_multiply_fusion
  24.9 2.0 copy-done.2
  26.9 1.4 convolution_select_fusion.2
  28.4 4.9 select_bitcast_fusion.2
  33.5 62.7 %all-reduce.7.cloned.1.call-done = f32[2,256,256]{2,1,0:T(8,128)} async-done(((f32[2,256,256]{2,1,0:T(8,128)}), f32[2,256,256]{2,1,0:T(8,128)}) %all-reduce.7.cloned.1.call-update) | async-done | bytes 524304 | tf_op jit(solution)/shard_map/psum | solution.py:11
  96.2 155.0 %all-reduce.9.cloned.1.call-done = f32[256,8,256]{2,0,1:T(8,128)} async-done(((f32[256,8,256]{2,0,1:T(8,128)}), f32[256,8,256]{2,0,1:T(8,128)}) %all-reduce.9.cloned.1.call-update) | async-done | bytes 2097168 | tf_op jit(solution)/shard_map/psum | solution.py:11
  251.2 7.1 multiply_subtract_fusion.2
  259.0 2.0 copy-done
  261.0 1.4 convolution_select_fusion.1
  262.7 4.3 select_bitcast_fusion.1
  267.1 60.8 %all-reduce.11.cloned.1.call-done = f32[2,256,256]{2,1,0:T(8,128)} async-done(((f32[2,256,256]{2,1,0:T(8,128)}), f32[2,256,256]{2,1,0:T(8,128)}) %all-reduce.11.cloned.1.call-update) | async-done | bytes 524304 | tf_op jit(solution)/shard_map/psum | solution.py:11
  327.9 154.9 %all-reduce.13.cloned.1.call-done = f32[256,8,256]{2,0,1:T(8,128)} async-done(((f32[256,8,256]{2,0,1:T(8,128)}), f32[256,8,256]{2,0,1:T(8,128)}) %all-reduce.13.cloned.1.call-update) | async-done | bytes 2097168 | tf_op jit(solution)/shard_map/psum | solution.py:11
  482.8 7.1 multiply_subtract_fusion.1
  490.6 2.0 copy-done.1
  492.6 1.4 convolution_select_fusion
  494.3 4.3 select_bitcast_fusion
  498.7 60.9 %all-reduce.15.cloned.1.call-done = f32[2,256,256]{2,1,0:T(8,128)} async-done(((f32[2,256,256]{2,1,0:T(8,128)}), f32[2,256,256]{2,1,0:T(8,128)}) %all-reduce.15.cloned.1.call-update) | async-done | bytes 524304 | tf_op jit(solution)/shard_map/psum | solution.py:11
  559.5 154.9 %all-reduce.17.cloned.1.call-done = f32[256,8,256]{2,0,1:T(8,128)} async-done(((f32[256,8,256]{2,0,1:T(8,128)}), f32[256,8,256]{2,0,1:T(8,128)}) %all-reduce.17.cloned.1.call-update) | async-done | bytes 2097168 | tf_op jit(solution)/shard_map/psum | solution.py:11
  714.4 6.8 multiply_subtract_fusion
  721.9 4.4 copy.25
  (55 shorter events, 3.2 us)
Async XLA Ops:
  6.5 89.7 %all-reduce.7.cloned.1.call-start = ((), (), s32[]{:S(2)}) async-start(), calls=%async_computation | async-start | bytes 1048576 | tf_op jit(solution)/shard_map/psum | solution.py:11
  22.1 4.9 copy-start.9
  24.9 2.0 copy-start.2
  28.3 222.9 %all-reduce.9.cloned.1.call-start = ((), (), s32[]{:S(2)}) async-start(), calls=%async_computation.1 | async-start | bytes 4194304 | tf_op jit(solution)/shard_map/psum | solution.py:11
  33.3 294.6 %all-reduce.11.cloned.1.call-start = ((), (), s32[]{:S(2)}) async-start(), calls=%async_computation.2 | async-start | bytes 1048576 | tf_op jit(solution)/shard_map/psum | solution.py:11
  96.2 162.2 %copy-start.6 = (f32[2,256,256]{2,1,0:T(8,128)S(1)}, f32[2,256,256]{2,1,0:T(8,128)}, u32[]{:S(2)}) copy-start(f32[2,256,256]{2,1,0:T(8,128)} %all-reduce.7.cloned.1.call-done) | copy-start | bytes 1572868
  251.2 7.3 copy-start.3
  259.0 2.0 copy-start
  262.4 220.4 %all-reduce.13.cloned.1.call-start = ((), (), s32[]{:S(2)}) async-start(), calls=%async_computation.3 | async-start | bytes 4194304 | tf_op jit(solution)/shard_map/psum | solution.py:11
  267.0 292.6 %all-reduce.15.cloned.1.call-start = ((), (), s32[]{:S(2)}) async-start(), calls=%async_computation.4 | async-start | bytes 1048576 | tf_op jit(solution)/shard_map/psum | solution.py:11
  327.9 162.0 %copy-start.7 = (f32[2,256,256]{2,1,0:T(8,128)S(1)}, f32[2,256,256]{2,1,0:T(8,128)}, u32[]{:S(2)}) copy-start(f32[2,256,256]{2,1,0:T(8,128)} %all-reduce.11.cloned.1.call-done) | copy-start | bytes 1572868
  482.8 7.3 copy-start.4
  490.6 2.0 copy-start.1
  494.0 220.4 %all-reduce.17.cloned.1.call-start = ((), (), s32[]{:S(2)}) async-start(), calls=%async_computation.5 | async-start | bytes 4194304 | tf_op jit(solution)/shard_map/psum | solution.py:11
  559.5 161.7 %copy-start.8 = (f32[2,256,256]{2,1,0:T(8,128)S(1)}, f32[2,256,256]{2,1,0:T(8,128)}, u32[]{:S(2)}) copy-start(f32[2,256,256]{2,1,0:T(8,128)} %all-reduce.15.cloned.1.call-done) | copy-start | bytes 1572868
  714.4 7.0 copy-start.5
Sparse Core Ops, SparseCore 0:
  28.5 67.7 all-reduce.6
  100.1 151.0 all-reduce.8
  262.6 65.3 all-reduce.10
  331.7 151.0 all-reduce.12
  494.1 65.3 all-reduce.14
  563.3 151.0 all-reduce.16
where the time goes:
time: 737 us; the launch traced here: 733 us
  waiting for transfers between devices  649 us (88%)
  matrix products  39.8 us (5%)
  local copies, waits for them, and re-layouts  24.7 us (3%)
  between operations  13.7 us (2%)
    psum x6, waiting for transfers between devices, broadcast(): return lax.psum(jnp.where(mine, array, jnp.zeros_like(array)), axis)  649 us
    dot_general x3, matrix products, on_device(): jnp.einsum('irt,tjs->irjs', left_block, upper_block, precision=high)  21.1 us
  transfers between devices with their start and end apart: 6, of which 6 were waited for; matrix products, arithmetic and copies ran while one was open for 2% of the time, Pallas kernels for 0%

commit v1 on v0

v1 whole, which is shorter than its diff:
```python
import functools

import jax
import jax.numpy as jnp
from jax import lax
from jax.experimental import pallas as pl
from jax.experimental.pallas import tpu as pltpu

PANELS = 3
NX, NZ = 4, 8
SMEM = pltpu.SMEM
VMEM = pltpu.VMEM
F32 = jnp.float32
BF16 = jnp.bfloat16


def split(value):
    high = value.astype(BF16)
    return high, (value - high.astype(F32)).astype(BF16)


def dot3(a, b):
    (ah, al), (bh, bl) = a, b
    one = functools.partial(jnp.dot, preferred_element_type=F32)
    return one(ah, bh) + (one(ah, bl) + one(al, bh))


def params(mib=48):
    return pltpu.CompilerParams(vmem_limit_bytes=mib * 2**20)


def pack_body(m, quarters, where_ref, pattern_ref, perm_ref, a_ref, *rest):
    out_refs, moved = rest[:-1], rest[-1]
    prow, pcol, turn = where_ref[0], where_ref[1], where_ref[2]
    rows = a_ref.shape[1]
    cols = a_ref.shape[2]

    def move(r, carry):
        for u in range(8):
            moved[r * 8 + u] = a_ref[0, perm_ref[m, r * 8 + u]]
        return carry

    lax.fori_loop(0, rows // 8, move, 0)
    for c in range(cols):
        keep = pattern_ref[m * 32 + prow, c * 8 + pcol].astype(F32)
        block = moved[:, c, :] * keep
        if quarters:
            out_refs[0][c] = block
            part = rows // 4
            for slot in range(4):
                first = lax.rem(turn + slot, 4) * part
                piece = moved[pl.ds(first, part), c, :] * keep
                for h in range(2):
                    out_refs[1][slot, h, c] = piece[h * (part // 2) : (h + 1) * (part // 2)]
        else:
            out_refs[0][c] = block


def pack(m, quarters, where, pattern, perm, matrix):
    _, rows, cols, width = matrix.shape
    half = width // 2
    shapes = [jax.ShapeDtypeStruct((cols, rows, width), F32)]
    specs = [pl.BlockSpec((cols, rows, half), lambda i: (0, 0, i))]
    if quarters:
        shapes.append(jax.ShapeDtypeStruct((4, 2, cols, rows // 8, width), F32))
        specs.append(pl.BlockSpec((4, 2, cols, rows // 8, half), lambda i: (0, 0, 0, 0, i)))
    return pl.pallas_call(
        functools.partial(pack_body, m, quarters),
        grid=(2,),
        in_specs=[
            pl.BlockSpec(memory_space=SMEM),
            pl.BlockSpec(memory_space=SMEM),
            pl.BlockSpec(memory_space=SMEM),
            pl.BlockSpec((1, rows, cols, half), lambda i: (m, 0, 0, i)),
        ],
        out_specs=specs,
        out_shape=shapes,
        scratch_shapes=[VMEM((rows, cols, half), F32)],
        compiler_params=params(),
        name="pack",
    )(where, pattern, perm, matrix)


def left_body(
    where_ref, pattern_ref, cols_ref, corner_ref, linv_ref, uinv_ref,
    lh_ref, ll_ref, ch_ref, cl_ref, raw_ref, both,
):
    prow = where_ref[0]
    turn = where_ref[2]
    part = 64
    for q in range(3):
        for slot in range(4):
            shift = (0, 3, 1, 2)[slot]
            first = lax.rem(turn + shift, 4) * part
            for h in range(2):
                for row in range(2):
                    both[q, row, pl.ds(first + h * 32, 32), :] = corner_ref[q, slot, h, row]
    li = [split(linv_ref[k]) for k in range(2)]
    ui = [split(uinv_ref[k]) for k in range(3)]
    a10, a20 = both[0, 0], both[0, 1]
    a01, a21 = both[1, 0], both[1, 1]
    a02, a12 = both[2, 0], both[2, 1]
    u01 = split(dot3(li[0], split(a01)))
    u02 = split(dot3(li[0], split(a02)))
    l10 = split(dot3(split(a10), ui[0]))
    l20 = split(dot3(split(a20), ui[0]))
    p12 = pattern_ref[1, 2].astype(F32)
    p21 = pattern_ref[2, 1].astype(F32)
    u12 = split(dot3(li[1], split(a12 - p12 * dot3(l10, u02))))
    l21 = split(dot3(split(a21 - p21 * dot3(l20, u01)), ui[1]))
    for n, value in enumerate((l10, l20, l21)):
        ch_ref[n] = value[0]
        cl_ref[n] = value[1]
    for m in range(2):
        row = m * 32 + prow
        rows = pl.ds(m * 256, 256)
        l0 = dot3(split(cols_ref[0, m]), ui[0])
        l0s = split(l0)
        p1 = pattern_ref[row, 1].astype(F32)
        l1 = dot3(split(cols_ref[1, m] - p1 * dot3(l0s, u01)), ui[1])
        l1s = split(l1)
        p2 = pattern_ref[row, 2].astype(F32)
        l2 = dot3(
            split(cols_ref[2, m] - p2 * (dot3(l0s, u02) + dot3(l1s, u12))), ui[2]
        )
        for k, value in enumerate((l0, l1, l2)):
            raw_ref[k, m] = value
            live = jnp.where(row > k, value, 0.0)
            high, low = split(live)
            lh_ref[rows, pl.ds(k * 256, 256)] = high
            ll_ref[rows, pl.ds(k * 256, 256)] = low


def left(where, pattern, cols, corner, lower_inv, upper_inv):
    smem = pl.BlockSpec(memory_space=SMEM)
    vmem = pl.BlockSpec(memory_space=VMEM)
    return pl.pallas_call(
        left_body,
        in_specs=[smem, smem, vmem, vmem, vmem, vmem],
        out_specs=[vmem] * 5,
        out_shape=[
            jax.ShapeDtypeStruct((512, 768), BF16),
            jax.ShapeDtypeStruct((512, 768), BF16),
            jax.ShapeDtypeStruct((3, 256, 256), BF16),
            jax.ShapeDtypeStruct((3, 256, 256), BF16),
            jax.ShapeDtypeStruct((3, 2, 256, 256), F32),
        ],
        scratch_shapes=[VMEM((3, 2, 256, 256), F32)],
        compiler_params=params(),
        name="left",
    )(where, pattern, cols, corner, lower_inv, upper_inv)


def finish_body(
    where_ref, pattern_ref, ap0_ref, ap1_ref, lh_ref, ll_ref, ch_ref, cl_ref, raw_ref, linv_ref,
    *rest,
):
    first_refs, main_refs = rest[0:4], rest[4:12]
    out_ref, panel, upper = rest[12:]
    c = pl.program_id(0)
    prow, pcol, turn = where_ref[0], where_ref[1], where_ref[2]
    col = c * 8 + pcol
    shifts = (0, 3, 1, 2)

    @pl.when(c == 0)
    def _():
        for slot in range(4):
            first = lax.rem(turn + shifts[slot], 4) * 64
            for h in range(2):
                panel[:, pl.ds(first + h * 32, 32), :] = first_refs[slot][h]

    @pl.when(c > 0)
    def _():
        for slot in range(4):
            first = lax.rem(turn + shifts[slot], 4) * 64
            for h in range(2):
                panel[:, pl.ds(first + h * 32, 32), :] = main_refs[slot * 2 + h][:, 0]

    corner = [(ch_ref[n], cl_ref[n]) for n in range(3)]
    li = [split(linv_ref[k]) for k in range(3)]
    u0 = dot3(li[0], split(panel[0]))
    u0s = split(u0)
    p1 = pattern_ref[1, col].astype(F32)
    u1 = dot3(li[1], split(panel[1] - p1 * dot3(corner[0], u0s)))
    u1s = split(u1)
    p2 = pattern_ref[2, col].astype(F32)
    u2 = dot3(li[2], split(panel[2] - p2 * (dot3(corner[1], u0s) + dot3(corner[2], u1s))))
    u2s = split(u2)
    for k, value in enumerate((u0, u1, u2)):
        upper[k] = value
    uh = jnp.concatenate([u0s[0], u1s[0], u2s[0]], axis=0)
    ul = jnp.concatenate([u0s[1], u1s[1], u2s[1]], axis=0)
    total = dot3((lh_ref[...], ll_ref[...]), (uh, ul))
    for m, ap_ref in enumerate((ap0_ref, ap1_ref)):
        row = m * 32 + prow
        keep = pattern_ref[row, col].astype(F32)
        out_ref[m, :, c, :] = ap_ref[0] - keep * total[m * 256 : (m + 1) * 256]

        @pl.when(jnp.logical_and(col < 3, row > col))
        def _():
            out_ref[m, :, c, :] = raw_ref[jnp.minimum(col, 2), m]

        if m == 0:

            @pl.when(jnp.logical_and(row < 3, row < col))
            def _():
                out_ref[m, :, c, :] = upper[jnp.minimum(row, 2)]


def finish(where, pattern, ap0, ap1, lh, ll, ch, cl, raw, lower_inv, firsts, mains):
    smem = pl.BlockSpec(memory_space=SMEM)
    vmem = pl.BlockSpec(memory_space=VMEM)
    block = pl.BlockSpec((1, 256, 256), lambda c: (c, 0, 0))
    main = pl.BlockSpec((3, 1, 32, 256), lambda c: (0, jnp.maximum(c, 1) - 1, 0, 0))
    return pl.pallas_call(
        finish_body,
        grid=(8,),
        in_specs=[smem, smem, block, block] + [vmem] * 6 + [vmem] * 4 + [main] * 8,
        out_specs=pl.BlockSpec((2, 256, 8, 256), lambda c: (0, 0, 0, 0)),
        out_shape=jax.ShapeDtypeStruct((2, 256, 8, 256), F32),
        scratch_shapes=[VMEM((3, 256, 256), F32), VMEM((3, 256, 256), F32)],
        compiler_params=params(),
        name="finish",
    )(where, pattern, ap0, ap1, lh, ll, ch, cl, raw, lower_inv, *firsts, *mains)


def hop(array, step, sources):
    pairs = []
    for x in range(NX):
        for z in range(NZ):
            if sources(x, z):
                to = ((x + step[0]) % NX) * NZ + (z + step[1]) % NZ
                pairs.append((x * NZ + z, to))
    return lax.ppermute(array, "prow", pairs)


def on_device(matrix, pattern, row_perm, lower_inv, upper_inv):
    prow = lax.axis_index("prow")
    pcol = lax.axis_index("pcol")
    x, z = prow // NZ, prow % NZ
    turn = lax.rem(x + 2 * z, 4)
    where = jnp.stack([prow, pcol, turn]).astype(jnp.int32)
    ap0, cut = pack(0, True, where, pattern, row_perm, matrix)
    sent = [hop(cut[d], (d, 0), lambda x, z: x == 0 and z < 3) for d in (1, 3, 2)]
    (ap1,) = pack(1, False, where, pattern, row_perm, matrix)
    columns = lax.all_gather(jnp.stack([ap0[0], ap1[0]]), "pcol", axis=0)
    own = jnp.where(x == 0, cut[0], sent[0] + sent[1] + sent[2])
    far = hop(own, (0, 4), lambda x, z: z < 3)
    held = jnp.where(z < 4, own, far)
    some = lambda x, z: z % 4 < 3
    after = hop(held, (2, 1), some)
    before = hop(held, (2, -1), some)
    two = hop(held, (0, 2), some)
    phase = z % 4

    def row(r, part):
        return jnp.where(
            phase == r, held[part], jnp.where(phase == (r + 1) % 4, after[part], jnp.where(phase == (r + 3) % 4, before[part], two[part]))
        )

    every = lambda x, z: True
    start = jnp.stack([jnp.stack([row(r, (h, 0)) for r in range(3)]) for h in range(2)])
    mine = [jnp.stack([row(r, (h, slice(1, None))) for r in range(3)]) for h in range(2)]
    firsts = [
        start,
        hop(start, (1, 0), every),
        hop(start, (-1, 0), every),
        hop(start, (0, 1), every),
    ]
    low = [jnp.where(pcol == 0, f[:, 1], f[:, 0]) for f in firsts]
    high = [jnp.where(pcol == 2, f[:, 1], f[:, 2]) for f in firsts]
    corner = jnp.stack([jnp.stack([a, b], axis=1) for a, b in zip(low, high)])
    corner = lax.all_gather(corner, "pcol", axis=0)[:3]
    mains = [mine[0], mine[1]]
    mains += [hop(mine[0], (1, 0), every), hop(mine[1], (1, 0), every)]
    mains += [hop(mine[0], (-1, 0), every), hop(mine[1], (-1, 0), every)]
    mains += [hop(mine[0], (0, 1), every), hop(mine[1], (0, -1), every)]
    lh, ll, ch, cl, raw = left(where, pattern, columns[:3], corner, lower_inv, upper_inv)
    return finish(where, pattern, ap0, ap1, lh, ll, ch, cl, raw, lower_inv, firsts, mains)


def solution(mesh):
    P = jax.sharding.PartitionSpec
    in_specs = (P(None, "prow", None, "pcol"), P(), P(None, "prow"), P(), P())
    out_specs = P(None, "prow", None, "pcol")
    return jax.shard_map(
        on_device, mesh=mesh, in_specs=in_specs, out_specs=out_specs, check_vma=False
    )
```

time: 737 us -> 213 us (0.29)
  waiting for transfers between devices: 649 us -> 77.2 us
  starting transfers between devices: 0.61 us -> 60 us
  Pallas kernels: 0 us -> 42.9 us
  matrix products: 39.8 us -> 0 us
  local copies, waits for them, and re-layouts: 24.7 us -> 14.8 us
    psum x6 -> x0, waiting for transfers between devices: 649 us -> none  [broadcast(): return lax.psum(jnp.where(mine, array, jnp.zeros_like(array)), axis)]
    ppermute x0 -> x16, starting transfers between devices: none -> 59.9 us  [hop(): return lax.ppermute(array, 'prow', pairs)]
    ppermute x0 -> x16, waiting for transfers between devices: none -> 59.8 us  [hop(): return lax.ppermute(array, 'prow', pairs)]
    pallas_call x0 -> x4, Pallas kernels: none -> 42.9 us  [the longest x1 26 us: finish(): pl.pallas_call(finish_body, grid=(8,), in_specs=[smem, smem, block, block...]
    dot_general x11 -> x0, matrix products: 39.8 us -> none  [the longest x3 21.1 us: on_device(): jnp.einsum('irt,tjs->irjs', left_block, upper_block, precision=high)]
    all_gather x0 -> x2, waiting for transfers between devices: none -> 17.4 us  [the longest x1 17.4 us: on_device(): corner = lax.all_gather(corner, 'pcol', axis=0)[:3]]
    gather x2 -> x0, local copies, waits for them, and re-layouts: 13.5 us -> none  [on_device(): blocks = jax.vmap(lambda single, rows: single[rows])(matrix, row_perm)]
  transfers between devices with their start and end apart: 6 -> 18, of which waited for: 6 -> 11; matrix products, arithmetic and copies ran while one was open for 2% -> 5% of each run, Pallas kernels for 0% -> 3%
where the time goes in v1:
time: 213 us; the launch traced here: 212 us
  waiting for transfers between devices  77.2 us (36%)
  starting transfers between devices  60 us (28%)
  Pallas kernels  42.9 us (20%)
  local copies, waits for them, and re-layouts  14.8 us (7%)
  between operations  13.7 us (6%)
  other arithmetic  3.83 us (2%)
    ppermute x16, starting transfers between devices, hop(): return lax.ppermute(array, 'prow', pairs)  59.9 us
    ppermute x16, waiting for transfers between devices, hop(): return lax.ppermute(array, 'prow', pairs)  59.8 us
    pallas_call x1, Pallas kernels, finish(): pl.pallas_call(finish_body, grid=(8,), in_specs=[smem, smem, block, block...  26 us
    all_gather x1, waiting for transfers between devices, on_device(): corner = lax.all_gather(corner, 'pcol', axis=0)[:3]  17.4 us
    pallas_call x2, Pallas kernels, pack(): pl.pallas_call(functools.partial(pack_body, m, quarters), grid=(2,), in_s...  11.3 us
    unnamed x26, local copies, waits for them, and re-layouts  8.04 us
    pallas_call x1, Pallas kernels, left(): pl.pallas_call(left_body, in_specs=[smem, smem, vmem, vmem, vmem, vmem],...  5.67 us
  transfers between devices with their start and end apart: 18, of which 11 were waited for; matrix products, arithmetic and copies ran while one was open for 5% of the time, Pallas kernels for 3%

profile of v1, /device:TPU:1, one launch (start us, length us, event | category | flops | bytes accessed | tf_op | source)
XLA Modules:
  0.0 212.4 jit_solution(4012615172679242939)
XLA Ops:
  8.1 4.5 %pack.3.ap1_ref = f32[8,256,256]{2,1,0:T(8,128)S(1)} custom-call(s32[3]{0:T(128)S(1)} %pad_add_fusion.where_ref, s32[64,64]{1,0:T(8,128)S(1)} %copy-done.9, s32[2,256]{1,0:T(2,128)S(1)} %copy-done.11, f32[2,256,8,256]{3,2,1,0:T(8,128)} %a_ref.3), custom_call_target="tpu_custom_call" | custom-call | tf_op jit(solution)/shard_map/pack/pallas_call | solution.py:67
  12.6 6.8 %pack.2 = (f32[8,256,256]{2,1,0:T(8,128)S(1)}, f32[4,2,8,32,256]{4,3,2,1,0:T(8,128)S(1)}) custom-call(s32[3]{0:T(128)S(1)} %pad_add_fusion.where_ref, s32[64,64]{1,0:T(8,128)S(1)} %copy-done.9, s32[2,256]{1,0:T(2,128)S(1)} %copy-done.11, f32[2,256,8,256]{3,2,1,0:T(8,128)} %a_ref.3), custom_call_target="tpu_custom_call" | custom-call | tf_op jit(solution)/shard_map/pack/pallas_call | solution.py:67
  24.2 5.2 %collective-permute-start.1 = (f32[2,8,32,256]{3,2,1,0:T(8,128)}, f32[2,8,32,256]{3,2,1,0:T(8,128)S(1)}, u32[]{:S(2)}, u32[]{:S(2)}) collective-permute-start(f32[2,8,32,256]{3,2,1,0:T(8,128)} %get-tuple-element.31), channel_id=1, source_target_pairs={{0,192},{8,200},{16,208},{1,193},{9,201},{17,209},{2,194},{10,202}... | collective-permute-start | bytes 1572872 | tf_op jit(solution)/shard_map/ppermute | solution.py:234
  29.4 2.1 collective-permute-start.2
  31.5 2.1 collective-permute-start
  33.6 6.7 %collective-permute-done.1 = f32[2,8,32,256]{3,2,1,0:T(8,128)S(1)} collective-permute-done((f32[2,8,32,256]{3,2,1,0:T(8,128)}, f32[2,8,32,256]{3,2,1,0:T(8,128)S(1)}, u32[]{:S(2)}, u32[]{:S(2)}) %collective-permute-start.1) | collective-permute-done | bytes 524320 | tf_op jit(solution)/shard_map/ppermute | solution.py:234
  41.6 11.1 %collective-permute-done = f32[2,8,32,256]{3,2,1,0:T(8,128)} collective-permute-done((f32[2,8,32,256]{3,2,1,0:T(8,128)S(1)}, f32[2,8,32,256]{3,2,1,0:T(8,128)}, u32[]{:S(2)}, u32[]{:S(2)}) %collective-permute-start) | collective-permute-done | bytes 524320 | tf_op jit(solution)/shard_map/ppermute | solution.py:234
  55.4 9.9 %collective-permute-done.3 = f32[2,8,32,256]{3,2,1,0:T(8,128)S(1)} collective-permute-done((f32[2,8,32,256]{3,2,1,0:T(8,128)S(1)}, f32[2,8,32,256]{3,2,1,0:T(8,128)S(1)}, u32[]{:S(2)}, u32[]{:S(2)}) %collective-permute-start.3) | collective-permute-done | bytes 524320 | tf_op jit(solution)/shard_map/ppermute | solution.py:234
  65.4 28.2 %collective-permute-start.6 = (f32[2,8,32,256]{3,2,1,0:T(8,128)S(1)}, f32[2,8,32,256]{3,2,1,0:T(8,128)S(1)}, u32[]{:S(2)}, u32[]{:S(2)}) collective-permute-start(f32[2,8,32,256]{3,2,1,0:T(8,128)S(1)} %broadcast_select_fusion), channel_id=1, source_target_pairs={{0,16},{8,24},{16,32},{32,48},{40,56},{48,0},{64,80},{72,88},{80,9... | collective-permute-start | bytes 1572872 | tf_op jit(solution)/shard_map/ppermute | solution.py:234
  93.6 1.9 collective-permute-start.5
  95.5 5.8 %collective-permute-start.4 = (f32[2,8,32,256]{3,2,1,0:T(8,128)S(1)}, f32[2,8,32,256]{3,2,1,0:T(8,128)S(1)}, u32[]{:S(2)}, u32[]{:S(2)}) collective-permute-start(f32[2,8,32,256]{3,2,1,0:T(8,128)S(1)} %broadcast_select_fusion), channel_id=1, source_target_pairs={{0,136},{8,144},{16,152},{32,168},{40,176},{48,184},{64,200},{72,2... | collective-permute-start | bytes 1572872 | tf_op jit(solution)/shard_map/ppermute | solution.py:234
  101.3 8.0 %collective-permute-done.6 = f32[2,8,32,256]{3,2,1,0:T(8,128)S(1)} collective-permute-done((f32[2,8,32,256]{3,2,1,0:T(8,128)S(1)}, f32[2,8,32,256]{3,2,1,0:T(8,128)S(1)}, u32[]{:S(2)}, u32[]{:S(2)}) %collective-permute-start.6) | collective-permute-done | bytes 524320 | tf_op jit(solution)/shard_map/ppermute | solution.py:234
  110.6 5.2 %collective-permute-done.4 = f32[2,8,32,256]{3,2,1,0:T(8,128)S(1)} collective-permute-done((f32[2,8,32,256]{3,2,1,0:T(8,128)S(1)}, f32[2,8,32,256]{3,2,1,0:T(8,128)S(1)}, u32[]{:S(2)}, u32[]{:S(2)}) %collective-permute-start.4) | collective-permute-done | bytes 524320 | tf_op jit(solution)/shard_map/ppermute | solution.py:234
  115.9 2.3 %collective-permute-start.7 = (f32[2,3,32,256]{3,2,1,0:T(8,128)S(1)}, f32[2,3,32,256]{3,2,1,0:T(8,128)S(1)}, u32[]{:S(2)}, u32[]{:S(2)}) collective-permute-start(f32[2,3,32,256]{3,2,1,0:T(8,128)S(1)} %pad_maximum_fusion.4.rest_0_), channel_id=1, source_target_pairs={{0,64},{8,72},{16,80},{24,88},{32,96},{40,104},{48,112},{56,120},{... | collective-permute-start | bytes 589832 | tf_op jit(solution)/shard_map/ppermute | solution.py:234
  118.6 3.9 %collective-permute-start.9 = (f32[2,3,32,256]{3,2,1,0:T(8,128)S(1)}, f32[2,3,32,256]{3,2,1,0:T(8,128)S(1)}, u32[]{:S(2)}, u32[]{:S(2)}) collective-permute-start(f32[2,3,32,256]{3,2,1,0:T(8,128)S(1)} %pad_maximum_fusion.4.rest_0_), channel_id=1, source_target_pairs={{0,8},{8,16},{16,24},{24,32},{32,40},{40,48},{48,56},{56,0},{64,72... | collective-permute-start | bytes 589832 | tf_op jit(solution)/shard_map/ppermute | solution.py:234
  123.0 6.5 %collective-permute-done.9.rest_3_ = f32[2,3,32,256]{3,2,1,0:T(8,128)S(1)} collective-permute-done((f32[2,3,32,256]{3,2,1,0:T(8,128)S(1)}, f32[2,3,32,256]{3,2,1,0:T(8,128)S(1)}, u32[]{:S(2)}, u32[]{:S(2)}) %collective-permute-start.9) | collective-permute-done | bytes 196640 | tf_op jit(solution)/shard_map/ppermute | solution.py:234
  132.6 2.7 %collective-permute-start.15 = (f32[3,7,32,256]{3,2,1,0:T(8,128)S(1)}, f32[3,7,32,256]{3,2,1,0:T(8,128)}, u32[]{:S(2)}, u32[]{:S(2)}) collective-permute-start(f32[3,7,32,256]{3,2,1,0:T(8,128)S(1)} %pad_maximum_fusion.1.rest_5_), channel_id=1, source_target_pairs={{0,56},{8,0},{16,8},{24,16},{32,24},{40,32},{48,40},{56,48},{64,12... | collective-permute-start | bytes 2064392 | tf_op jit(solution)/shard_map/ppermute | solution.py:234
  135.2 2.3 %collective-permute-start.13 = (f32[3,7,32,256]{3,2,1,0:T(8,128)S(1)}, f32[3,7,32,256]{3,2,1,0:T(8,128)}, u32[]{:S(2)}, u32[]{:S(2)}) collective-permute-start(f32[3,7,32,256]{3,2,1,0:T(8,128)S(1)} %pad_maximum_fusion.1.rest_5_), channel_id=1, source_target_pairs={{0,192},{8,200},{16,208},{24,216},{32,224},{40,232},{48,240},{56,2... | collective-permute-start | bytes 2064392 | tf_op jit(solution)/shard_map/ppermute | solution.py:234
  137.5 9.5 %collective-permute-done.14.rest_10_ = f32[3,7,32,256]{3,2,1,0:T(8,128)S(1)} collective-permute-done((f32[3,7,32,256]{3,2,1,0:T(8,128)S(1)}, f32[3,7,32,256]{3,2,1,0:T(8,128)S(1)}, u32[]{:S(2)}, u32[]{:S(2)}) %collective-permute-start.14) | collective-permute-done | bytes 688160 | tf_op jit(solution)/shard_map/ppermute | solution.py:234
  147.9 2.7 %slice.183 = f32[6,256,256]{2,1,0:T(8,128)} slice(f32[16,256,256]{2,1,0:T(8,128)} %all-gather.5.cloned.1.call-done), slice={[0:6], [0:256], [0:256]} | slice | bytes 3145728 | tf_op jit(solution)/shard_map/slice | solution.py:278
  150.7 17.4 %all-gather.7.cloned.1.call-done = f32[32,2,2,32,256]{4,3,2,1,0:T(8,128)} async-done(((f32[4,2,2,32,256]{4,3,2,1,0:T(8,128)}), f32[32,2,2,32,256]{4,3,2,1,0:T(8,128)}) %all-gather.7.cloned.1.call-update) | async-done | bytes 4194320 | tf_op jit(solution)/shard_map/all_gather | solution.py:273
  168.1 2.8 %slice.207 = f32[12,2,2,32,256]{4,3,2,1,0:T(8,128)} slice(f32[32,2,2,32,256]{4,3,2,1,0:T(8,128)} %all-gather.7.cloned.1.call-done), slice={[0:12], [0:2], [0:2], [0:32], [0:256]} | slice | bytes 3145728 | tf_op jit(solution)/shard_map/slice | solution.py:273
  170.9 5.7 %left.1 = (bf16[512,768]{1,0:T(8,128)(2,1)S(1)}, bf16[512,768]{1,0:T(8,128)(2,1)S(1)}, bf16[3,256,256]{2,1,0:T(8,128)(2,1)S(1)}, bf16[3,256,256]{2,1,0:T(8,128)(2,1)S(1)}, f32[3,2,256,256]{3,2,1,0:T(8,128)S(1)}) custom-call(s32[3]{0:T(128)S(1)} %pad_add_fusion.where_ref, s32[64,64]{1,0:T(8,128)S(1)} %copy-done.10, f32[3,2,256,256]{3,2,1,0:T(8,128)} %bitcast.37, ...), custom_call_target="tpu_custom_call" | custom-call | tf_op jit(solution)/shard_map/left/pallas_call | solution.py:137
  179.6 26.0 %finish.1 = f32[2,256,8,256]{3,2,1,0:T(8,128)} custom-call(s32[3]{0:T(128)S(1)} %pad_add_fusion.where_ref, s32[64,64]{1,0:T(8,128)S(1)} %copy-done.10, f32[8,256,256]{2,1,0:T(8,128)} %copy-done.2, f32[8,256,256]{2,1,0:T(8,128)} %copy-done, bf16[512,768]{1,0:T(8,128)(2,1)} %copy-done.6, bf16[512,768]{1,0:T(8,128)(2,1)} %copy-done.7, ...), custom_call_target="tpu_custom_call" | custom-call | tf_op jit(solution)/shard_map/finish/pallas_call | solution.py:215
  (70 shorter events, 19.4 us)
Async XLA Ops:
  6.5 141.4 %all-gather.5.cloned.1.call-start = ((), (), s32[]{:S(2)}) async-start(), calls=%async_computation | async-start | bytes 4718592 | tf_op jit(solution)/shard_map/all_gather | solution.py:246
  12.5 6.8 %copy-start = (f32[8,256,256]{2,1,0:T(8,128)}, f32[8,256,256]{2,1,0:T(8,128)S(1)}, u32[]{:S(2)}) copy-start(f32[8,256,256]{2,1,0:T(8,128)S(1)} %pack.3.ap1_ref) | copy-start | bytes 6291460
  20.7 1.3 copy-start.2
  20.7 2.4 %copy-start.4 = (f32[4,2,8,32,256]{4,3,2,1,0:T(8,128)S(1)}, f32[4,2,8,32,256]{4,3,2,1,0:T(8,128)}, u32[]{:S(2)}) copy-start(f32[4,2,8,32,256]{4,3,2,1,0:T(8,128)} %copy-done.3) | copy-start | bytes 6291460
  22.9 145.2 %all-gather.7.cloned.1.call-start = ((), (), s32[]{:S(2)}) async-start(), calls=%async_computation.1 | async-start | bytes 4718592 | tf_op jit(solution)/shard_map/all_gather | solution.py:273
  24.2 16.1 %collective-permute-start.1 = (f32[2,8,32,256]{3,2,1,0:T(8,128)}, f32[2,8,32,256]{3,2,1,0:T(8,128)S(1)}, u32[]{:S(2)}, u32[]{:S(2)}) collective-permute-start(f32[2,8,32,256]{3,2,1,0:T(8,128)} %get-tuple-element.31), channel_id=1, source_target_pairs={{0,192},{8,200},{16,208},{1,193},{9,201},{17,209},{2,194},{10,202}... | collective-permute-start | bytes 1572872 | tf_op jit(solution)/shard_map/ppermute | solution.py:234
  29.4 12.2 %collective-permute-start.2 = (f32[2,8,32,256]{3,2,1,0:T(8,128)}, f32[2,8,32,256]{3,2,1,0:T(8,128)}, u32[]{:S(2)}, u32[]{:S(2)}) collective-permute-start(f32[2,8,32,256]{3,2,1,0:T(8,128)} %get-tuple-element.32), channel_id=1, source_target_pairs={{0,128},{8,136},{16,144},{1,129},{9,137},{17,145},{2,130},{10,138}... | collective-permute-start | bytes 1572872 | tf_op jit(solution)/shard_map/ppermute | solution.py:234
  31.5 21.2 %collective-permute-start = (f32[2,8,32,256]{3,2,1,0:T(8,128)S(1)}, f32[2,8,32,256]{3,2,1,0:T(8,128)}, u32[]{:S(2)}, u32[]{:S(2)}) collective-permute-start(f32[2,8,32,256]{3,2,1,0:T(8,128)S(1)} %get-tuple-element.33), channel_id=1, source_target_pairs={{0,64},{8,72},{16,80},{1,65},{9,73},{17,81},{2,66},{10,74},{18,82}... | collective-permute-start | bytes 1572872 | tf_op jit(solution)/shard_map/ppermute | solution.py:234
  54.1 11.2 %collective-permute-start.3 = (f32[2,8,32,256]{3,2,1,0:T(8,128)S(1)}, f32[2,8,32,256]{3,2,1,0:T(8,128)S(1)}, u32[]{:S(2)}, u32[]{:S(2)}) collective-permute-start(f32[2,8,32,256]{3,2,1,0:T(8,128)S(1)} %bitcast_select_fusion), channel_id=1, source_target_pairs={{0,32},{8,40},{16,48},{64,96},{72,104},{80,112},{128,160},{136,168... | collective-permute-start | bytes 1572872 | tf_op jit(solution)/shard_map/ppermute | solution.py:234
  65.4 43.9 %collective-permute-start.6 = (f32[2,8,32,256]{3,2,1,0:T(8,128)S(1)}, f32[2,8,32,256]{3,2,1,0:T(8,128)S(1)}, u32[]{:S(2)}, u32[]{:S(2)}) collective-permute-start(f32[2,8,32,256]{3,2,1,0:T(8,128)S(1)} %broadcast_select_fusion), channel_id=1, source_target_pairs={{0,16},{8,24},{16,32},{32,48},{40,56},{48,0},{64,80},{72,88},{80,9... | collective-permute-start | bytes 1572872 | tf_op jit(solution)/shard_map/ppermute | solution.py:234
  93.6 17.0 %collective-permute-start.5 = (f32[2,8,32,256]{3,2,1,0:T(8,128)S(1)}, f32[2,8,32,256]{3,2,1,0:T(8,128)S(1)}, u32[]{:S(2)}, u32[]{:S(2)}) collective-permute-start(f32[2,8,32,256]{3,2,1,0:T(8,128)S(1)} %broadcast_select_fusion), channel_id=1, source_target_pairs={{0,184},{8,128},{16,136},{32,152},{40,160},{48,168},{64,248},{72,1... | collective-permute-start | bytes 1572872 | tf_op jit(solution)/shard_map/ppermute | solution.py:234
  95.5 20.3 %collective-permute-start.4 = (f32[2,8,32,256]{3,2,1,0:T(8,128)S(1)}, f32[2,8,32,256]{3,2,1,0:T(8,128)S(1)}, u32[]{:S(2)}, u32[]{:S(2)}) collective-permute-start(f32[2,8,32,256]{3,2,1,0:T(8,128)S(1)} %broadcast_select_fusion), channel_id=1, source_target_pairs={{0,136},{8,144},{16,152},{32,168},{40,176},{48,184},{64,200},{72,2... | collective-permute-start | bytes 1572872 | tf_op jit(solution)/shard_map/ppermute | solution.py:234
  115.9 6.7 %collective-permute-start.7 = (f32[2,3,32,256]{3,2,1,0:T(8,128)S(1)}, f32[2,3,32,256]{3,2,1,0:T(8,128)S(1)}, u32[]{:S(2)}, u32[]{:S(2)}) collective-permute-start(f32[2,3,32,256]{3,2,1,0:T(8,128)S(1)} %pad_maximum_fusion.4.rest_0_), channel_id=1, source_target_pairs={{0,64},{8,72},{16,80},{24,88},{32,96},{40,104},{48,112},{56,120},{... | collective-permute-start | bytes 589832 | tf_op jit(solution)/shard_map/ppermute | solution.py:234
  118.2 4.8 %collective-permute-start.8 = (f32[2,3,32,256]{3,2,1,0:T(8,128)S(1)}, f32[2,3,32,256]{3,2,1,0:T(8,128)S(1)}, u32[]{:S(2)}, u32[]{:S(2)}) collective-permute-start(f32[2,3,32,256]{3,2,1,0:T(8,128)S(1)} %pad_maximum_fusion.4.rest_0_), channel_id=1, source_target_pairs={{0,192},{8,200},{16,208},{24,216},{32,224},{40,232},{48,240},{56,2... | collective-permute-start | bytes 589832 | tf_op jit(solution)/shard_map/ppermute | solution.py:234
  118.6 10.9 %collective-permute-start.9 = (f32[2,3,32,256]{3,2,1,0:T(8,128)S(1)}, f32[2,3,32,256]{3,2,1,0:T(8,128)S(1)}, u32[]{:S(2)}, u32[]{:S(2)}) collective-permute-start(f32[2,3,32,256]{3,2,1,0:T(8,128)S(1)} %pad_maximum_fusion.4.rest_0_), channel_id=1, source_target_pairs={{0,8},{8,16},{16,24},{24,32},{32,40},{40,48},{48,56},{56,0},{64,72... | collective-permute-start | bytes 589832 | tf_op jit(solution)/shard_map/ppermute | solution.py:234
  130.9 16.2 %collective-permute-start.14 = (f32[3,7,32,256]{3,2,1,0:T(8,128)S(1)}, f32[3,7,32,256]{3,2,1,0:T(8,128)S(1)}, u32[]{:S(2)}, u32[]{:S(2)}) collective-permute-start(f32[3,7,32,256]{3,2,1,0:T(8,128)S(1)} %pad_maximum_fusion.rest_4_), channel_id=1, source_target_pairs={{0,8},{8,16},{16,24},{24,32},{32,40},{40,48},{48,56},{56,0},{64,72... | collective-permute-start | bytes 2064392 | tf_op jit(solution)/shard_map/ppermute | solution.py:234
  130.9 48.6 %collective-permute-start.12 = (f32[3,7,32,256]{3,2,1,0:T(8,128)S(1)}, f32[3,7,32,256]{3,2,1,0:T(8,128)}, u32[]{:S(2)}, u32[]{:S(2)}) collective-permute-start(f32[3,7,32,256]{3,2,1,0:T(8,128)S(1)} %pad_maximum_fusion.rest_4_), channel_id=1, source_target_pairs={{0,192},{8,200},{16,208},{24,216},{32,224},{40,232},{48,240},{56,2... | collective-permute-start | bytes 2064392 | tf_op jit(solution)/shard_map/ppermute | solution.py:234
  132.1 47.4 %collective-permute-start.10 = (f32[3,7,32,256]{3,2,1,0:T(8,128)S(1)}, f32[3,7,32,256]{3,2,1,0:T(8,128)}, u32[]{:S(2)}, u32[]{:S(2)}) collective-permute-start(f32[3,7,32,256]{3,2,1,0:T(8,128)S(1)} %pad_maximum_fusion.rest_4_), channel_id=1, source_target_pairs={{0,64},{8,72},{16,80},{24,88},{32,96},{40,104},{48,112},{56,120},{... | collective-permute-start | bytes 2064392 | tf_op jit(solution)/shard_map/ppermute | solution.py:234
  132.6 47.0 %collective-permute-start.15 = (f32[3,7,32,256]{3,2,1,0:T(8,128)S(1)}, f32[3,7,32,256]{3,2,1,0:T(8,128)}, u32[]{:S(2)}, u32[]{:S(2)}) collective-permute-start(f32[3,7,32,256]{3,2,1,0:T(8,128)S(1)} %pad_maximum_fusion.1.rest_5_), channel_id=1, source_target_pairs={{0,56},{8,0},{16,8},{24,16},{32,24},{40,32},{48,40},{56,48},{64,12... | collective-permute-start | bytes 2064392 | tf_op jit(solution)/shard_map/ppermute | solution.py:234
  135.2 44.3 %collective-permute-start.13 = (f32[3,7,32,256]{3,2,1,0:T(8,128)S(1)}, f32[3,7,32,256]{3,2,1,0:T(8,128)}, u32[]{:S(2)}, u32[]{:S(2)}) collective-permute-start(f32[3,7,32,256]{3,2,1,0:T(8,128)S(1)} %pad_maximum_fusion.1.rest_5_), channel_id=1, source_target_pairs={{0,192},{8,200},{16,208},{24,216},{32,224},{40,232},{48,240},{56,2... | collective-permute-start | bytes 2064392 | tf_op jit(solution)/shard_map/ppermute | solution.py:234
  147.9 31.7 %collective-permute-start.11 = (f32[3,7,32,256]{3,2,1,0:T(8,128)S(1)}, f32[3,7,32,256]{3,2,1,0:T(8,128)}, u32[]{:S(2)}, u32[]{:S(2)}) collective-permute-start(f32[3,7,32,256]{3,2,1,0:T(8,128)S(1)} %pad_maximum_fusion.1.rest_5_), channel_id=1, source_target_pairs={{0,64},{8,72},{16,80},{24,88},{32,96},{40,104},{48,112},{56,120},{... | collective-permute-start | bytes 2064392 | tf_op jit(solution)/shard_map/ppermute | solution.py:234
  150.7 20.2 %copy-start.1 = (f32[3,256,256]{2,1,0:T(8,128)S(1)}, f32[3,256,256]{2,1,0:T(8,128)}, u32[]{:S(2)}) copy-start(f32[3,256,256]{2,1,0:T(8,128)} %linv_ref.3) | copy-start | bytes 2359300
  150.7 20.2 %copy-start.10 = (s32[64,64]{1,0:T(8,128)S(1)}, s32[64,64]{1,0:T(8,128)}, u32[]{:S(2)}) copy-start(s32[64,64]{1,0:T(8,128)} %pattern_ref.7) | copy-start | bytes 49156
  168.1 2.9 %copy-start.8 = (f32[3,256,256]{2,1,0:T(8,128)S(1)}, f32[3,256,256]{2,1,0:T(8,128)}, u32[]{:S(2)}) copy-start(f32[3,256,256]{2,1,0:T(8,128)} %uinv_ref.1) | copy-start | bytes 2359300
  (7 other events, 6.6 us)
Sparse Core Ops, SparseCore 0:
  23.0 38.8 all-gather.4
  130.6 37.4 all-gather.6

commit v2 on v0

v2 whole, which is shorter than its diff:
```python
import functools

import jax
import jax.numpy as jnp
from jax import lax
from jax.experimental import pallas as pl
from jax.experimental.pallas import tpu as pltpu

NX, NZ = 4, 8
SHIFTS = (0, 3, 1, 2)
SMEM = pl.BlockSpec(memory_space=pltpu.SMEM)
ANY = pl.BlockSpec(memory_space=pl.ANY)
HERE = pl.BlockSpec(memory_space=pltpu.VMEM)
VMEM = pltpu.VMEM
F32 = jnp.float32
BF16 = jnp.bfloat16
shaped = jax.ShapeDtypeStruct


def params(mib):
    return pltpu.CompilerParams(vmem_limit_bytes=mib * 2**20)


def split(value):
    high = value.astype(BF16)
    return high, (value - high.astype(F32)).astype(BF16)


def wide(value):
    high, low = split(value)
    return jnp.concatenate([high, high, low], axis=1)


def tall(value):
    high, low = split(value)
    return jnp.concatenate([high, low, high], axis=0)


def dot(a, b):
    return jnp.dot(a, b, preferred_element_type=F32)


def gather_rows(m, perm_ref, source, moved):
    def move(r, carry):
        for u in range(16):
            moved[r * 16 + u] = source[perm_ref[m, r * 16 + u]]
        return carry

    lax.fori_loop(0, 16, move, 0)


def block_of(m, c, where_ref, pattern_ref, moved):
    keep = pattern_ref[m * 32 + where_ref[0], c * 8 + where_ref[1]].astype(F32)
    return moved[:, c, :] * keep


def pack_first_body(
    where_ref, pattern_ref, perm_ref, a_ref, faces_ref, m0, m1, m2, m3, raw, moved, packed, sem,
):
    loads = [
        pltpu.make_async_copy(
            a_ref.at[m, pl.ds(n * 64, 64)], raw.at[m, pl.ds(n * 64, 64)], sem.at[m * 4 + n]
        )
        for m in range(2)
        for n in range(4)
    ]
    for load in loads:
        load.start()
    for load in loads[:4]:
        load.wait()
    gather_rows(0, perm_ref, raw.at[0], moved)
    copies = []

    def copy(source, target):
        one = pltpu.make_async_copy(source, target, sem.at[8 + len(copies)])
        one.start()
        copies.append(one)

    def face(m, block):
        for j in range(8):
            copy(packed.at[block, pl.ds(j * 32, 32)], faces_ref.at[j, m])

    mains = (m0, m1, m2, m3)
    turn = where_ref[2]
    starts = [pl.multiple_of(lax.rem(turn + slot, 4) * 64, 64) for slot in range(4)]
    for c in range(8):
        packed[c] = block_of(0, c, where_ref, pattern_ref, moved)
        if c == 0:
            face(0, 0)
        if c % 4 == 3:
            part = pl.ds(c - 3, 4)
            for slot in (2, 1, 3, 0):
                for h in range(2):
                    rows = pl.ds(starts[slot] + h * 32, 32)
                    copy(packed.at[part, rows], mains[slot].at[h, part])
    for load in loads[4:]:
        load.wait()
    gather_rows(1, perm_ref, raw.at[1], moved)
    packed[8] = block_of(1, 0, where_ref, pattern_ref, moved)
    face(1, 8)
    for one in copies:
        one.wait()


def pack_first(where, pattern, perm, matrix):
    return pl.pallas_call(
        pack_first_body,
        in_specs=[SMEM, SMEM, SMEM, ANY],
        out_specs=[ANY] * 5,
        out_shape=[shaped((8, 2, 32, 256), F32)] + [shaped((2, 8, 32, 256), F32)] * 4,
        scratch_shapes=[
            VMEM((2, 256, 8, 256), F32),
            VMEM((256, 8, 256), F32),
            VMEM((9, 256, 256), F32),
            pltpu.SemaphoreType.DMA((40,)),
        ],
        compiler_params=params(58),
        name="pack_first",
    )(where, pattern, perm, matrix)


def pack_body(where_ref, pattern_ref, perm_ref, a_ref, after_ref, out0_ref, out1_ref, moved):
    for m, out_ref in enumerate((out0_ref, out1_ref)):
        gather_rows(m, perm_ref, a_ref.at[m], moved)
        for c in range(8):
            out_ref[c] = block_of(m, c, where_ref, pattern_ref, moved)


def pack(where, pattern, perm, matrix, after):
    return pl.pallas_call(
        pack_body,
        in_specs=[SMEM, SMEM, SMEM, HERE, ANY],
        out_specs=[HERE, HERE],
        out_shape=[shaped((8, 256, 256), F32)] * 2,
        scratch_shapes=[VMEM((256, 8, 256), F32)],
        compiler_params=params(20),
        name="pack",
    )(where, pattern, perm, matrix, after)


def merge_body(
    found_ref, columns_ref, held0, held1, after, before, two0, two1,
    all_ref, half0, half1, corner_ref, slices, sem,
):
    eight = pl.ds(0, 8)
    waits = []
    for r in range(3):
        for h in range(2):
            n = (r * 2 + h) * 3
            found = found_ref[r * 2 + h]
            sources = ((held0, held1)[h], after.at[h], before.at[h], (two0, two1)[h])

            def copies(source, n=n, r=r, h=h):
                return [
                    pltpu.make_async_copy(source.at[8], slices.at[r, h], sem.at[n]),
                    pltpu.make_async_copy(source.at[eight], all_ref.at[h, r], sem.at[n + 1]),
                    pltpu.make_async_copy(source.at[eight], (half0, half1)[h].at[r], sem.at[n + 2]),
                ]

            for which, source in enumerate(sources):

                @pl.when(found == which)
                def _():
                    for one in copies(source):
                        one.start()

            waits.append(copies(sources[0]))
    for group in waits:
        group[0].wait()
    last = [
        pltpu.make_async_copy(slices, corner_ref.at[q], sem.at[18 + q]) for q in range(8)
    ]
    for one in last:
        one.start()
    for group in waits:
        group[1].wait()
        group[2].wait()
    for one in last:
        one.wait()


def merge(found, columns, *parts):
    half = shaped((3, 8, 32, 256), F32)
    return pl.pallas_call(
        merge_body,
        in_specs=[SMEM] + [ANY] * 7,
        out_specs=[ANY] * 4,
        out_shape=[
            shaped((2, 3, 8, 32, 256), F32), half, half, shaped((8, 3, 2, 32, 256), F32)
        ],
        scratch_shapes=[VMEM((3, 2, 32, 256), F32), pltpu.SemaphoreType.DMA((26,))],
        compiler_params=params(8),
        name="merge",
    )(found, columns, *parts)


def left_body(
    where_ref, pattern_ref, columns_ref, corner_ref, linv_ref, uinv_ref,
    ll_ref, c3_ref, li_ref, raw_ref, column, both, linv, uinv, sem,
):
    prow = where_ref[0]
    copies = [
        pltpu.make_async_copy(linv_ref, linv, sem.at[0]),
        pltpu.make_async_copy(uinv_ref, uinv, sem.at[1]),
    ]
    for q in range(8):
        rows = pl.ds(q * 32, 32)
        copies.append(pltpu.make_async_copy(corner_ref.at[q], both.at[:, :, rows], sem.at[2 + q]))
        copies.append(pltpu.make_async_copy(columns_ref.at[q], column.at[:, :, rows], sem.at[10 + q]))
    for one in copies:
        one.start()
    for one in copies:
        one.wait()
    li = [wide(linv[k]) for k in range(3)]
    ui = [tall(uinv[k]) for k in range(3)]
    for k in range(3):
        li_ref[k] = li[k]
    a01, a02 = both[0, 0], both[0, 1]
    a10, a12 = both[1, 0], both[1, 1]
    a20, a21 = both[2, 0], both[2, 1]
    u01 = tall(dot(li[0], tall(a01)))
    u02 = tall(dot(li[0], tall(a02)))
    l10 = wide(dot(wide(a10), ui[0]))
    l20 = wide(dot(wide(a20), ui[0]))
    p12 = pattern_ref[1, 2].astype(F32)
    p21 = pattern_ref[2, 1].astype(F32)
    u12 = tall(dot(li[1], tall(a12 - p12 * dot(l10, u02))))
    l21 = wide(dot(wide(a21 - p21 * dot(l20, u01)), ui[1]))
    for n, value in enumerate((l10, l20, l21)):
        c3_ref[n] = value
    for m in range(2):
        row = m * 32 + prow
        rows = pl.ds(m * 256, 256)
        l0 = dot(wide(column[0, m]), ui[0])
        l0w = wide(l0)
        p1 = pattern_ref[row, 1].astype(F32)
        l1 = dot(wide(column[1, m] - p1 * dot(l0w, u01)), ui[1])
        l1w = wide(l1)
        p2 = pattern_ref[row, 2].astype(F32)
        l2 = dot(wide(column[2, m] - p2 * (dot(l0w, u02) + dot(l1w, u12))), ui[2])
        for k, value in enumerate((l0, l1, l2)):
            raw_ref[k, m] = value
            high, low = split(jnp.where(row > k, value, 0.0))
            ll_ref[rows, pl.ds(k * 768, 256)] = high
            ll_ref[rows, pl.ds(k * 768 + 256, 256)] = high
            ll_ref[rows, pl.ds(k * 768 + 512, 256)] = low


def left(where, pattern, columns, corner, lower_inv, upper_inv):
    outs = [
        shaped((512, 2304), BF16),
        shaped((3, 256, 768), BF16),
        shaped((3, 256, 768), BF16),
        shaped((3, 2, 256, 256), F32),
    ]
    return pl.pallas_call(
        left_body,
        in_specs=[SMEM, SMEM, ANY, ANY, ANY, ANY],
        out_specs=[HERE] * 4,
        out_shape=outs,
        scratch_shapes=[
            VMEM((3, 2, 256, 256), F32),
            VMEM((3, 2, 256, 256), F32),
            VMEM((3, 256, 256), F32),
            VMEM((3, 256, 256), F32),
            pltpu.SemaphoreType.DMA((18,)),
        ],
        compiler_params=params(20),
        name="left",
    )(where, pattern, columns, corner, lower_inv, upper_inv)


RANGES = ((0, 4), (4, 8))


def finish_body(
    where_ref, pattern_ref, ap0, ap1, ll, c3, li, raw, mine, lower, higher, half0, half1,
    out_ref, panel, upper, out, sem,
):
    prow, pcol, turn = where_ref[0], where_ref[1], where_ref[2]
    count = [0]

    def copy(source, target):
        one = pltpu.make_async_copy(source, target, sem.at[count[0]])
        count[0] += 1
        one.start()
        return one

    starts = [pl.multiple_of(lax.rem(turn + s, 4) * 64, 64) for s in SHIFTS]
    halves = [ref.at[h] for ref in (mine, lower, higher) for h in range(2)] + [half0, half1]

    def panels(n):
        lo, hi = RANGES[n]
        part = pl.ds(lo, hi - lo)
        for slot in range(4):
            for h in range(2):
                rows = pl.ds(starts[slot] + h * 32, 32)
                yield copy(halves[slot * 2 + h].at[:, part], panel.at[:, part, rows])

    def wait(group):
        for one in group:
            one.wait()

    def keep(i, c):
        return pattern_ref[i, c * 8 + pcol].astype(F32)

    def keeps(k, group):
        return jnp.concatenate([jnp.full((1, 256), keep(k, c), F32) for c in group], axis=1)

    def block(k, group):
        return jnp.concatenate([panel[k, c] for c in group], axis=1)

    def done(k, group, value):
        for n, c in enumerate(group):
            panel[k, c] = value[:, n * 256 : (n + 1) * 256]
        value = tall(value)
        upper[pl.ds(k * 768, 768), pl.ds(group[0] * 256, len(group) * 256)] = value
        return value

    def stages(group):
        u0 = done(0, group, dot(li[0], tall(block(0, group))))
        yield
        both = dot(c3[pl.ds(0, 2)].reshape(512, 768), u0)
        value = block(1, group) - keeps(1, group) * both[:256]
        u1 = done(1, group, dot(li[1], tall(value)))
        yield
        both = both[256:] + dot(c3[2], u1)
        value = block(2, group) - keeps(2, group) * both
        done(2, group, dot(li[2], tall(value)))
        yield

    def fix(m):
        @pl.when(jnp.logical_and(pcol < 3, m * 32 + prow > pcol))
        def _():
            out[m, :, 0, :] = raw[jnp.minimum(pcol, 2), m]

        if m == 0:

            @pl.when(prow < 3)
            def _():
                mine = jnp.minimum(prow, 2)
                for c in range(8):

                    @pl.when(prow < c * 8 + pcol)
                    def _():
                        out[0, :, c, :] = panel[mine, c]

    def update(c, m):
        total = dot(ll[pl.ds(m * 256, 256), :], upper[:, pl.ds(c * 256, 256)])
        out[m, :, c, :] = (ap0, ap1)[m][c] - keep(m * 32 + prow, c) * total

    groups = [[*panels(n)] for n in range(2)]
    wait(groups[0])
    for _ in stages(range(4)):
        pass
    wait(groups[1])
    for n, _ in enumerate(stages(range(4, 8))):
        if n < 2:
            for c in range(4):
                update(c, n)
    for c in range(4, 8):
        update(c, 0)
    fix(0)
    last = [copy(out.at[0], out_ref.at[0])]
    for c in (4, 5, 6, 7):
        update(c, 1)
    fix(1)
    last.append(copy(out.at[1], out_ref.at[1]))
    wait(last)


def finish(where, pattern, ap0, ap1, ll, c3, li, raw, *mains):
    return pl.pallas_call(
        finish_body,
        in_specs=[SMEM, SMEM] + [HERE] * 6 + [ANY] * 5,
        out_specs=ANY,
        out_shape=shaped((2, 256, 8, 256), F32),
        scratch_shapes=[
            VMEM((3, 8, 256, 256), F32),
            VMEM((2304, 2048), BF16),
            VMEM((2, 256, 8, 256), F32),
            pltpu.SemaphoreType.DMA((48,)),
        ],
        compiler_params=params(32),
        name="finish",
    )(where, pattern, ap0, ap1, ll, c3, li, raw, *mains)


def hop(array, steps, sources=lambda x, z: True):
    pairs = []
    for x in range(NX):
        for z in range(NZ):
            if sources(x, z):
                step = steps[z] if len(steps) > 1 else steps[0]
                to = ((x + step[0]) % NX) * NZ + (z + step[1]) % NZ
                pairs.append((x * NZ + z, to))
    return lax.ppermute(array, "prow", pairs)


def to_all(array):
    count = lax.axis_size("pcol")
    return lax.all_to_all(jnp.broadcast_to(array, (count, *array.shape)), "pcol", 0, 0)


PICK = (
    ((0, 1, 3, 2, 0, 1, 3, 2), (0, 1, 3, 2, 0, 1, 3, 2)),
    ((2, 0, 1, 3, 2, 0, 1, 3), (2, 0, 1, 3, 2, 0, 1, 3)),
    ((3, 2, 0, 1, 3, 2, 0, 1), (1, 2, 0, 1, 3, 3, 2, 0)),
)


def on_device(matrix, pattern, row_perm, lower_inv, upper_inv):
    prow = lax.axis_index("prow")
    pcol = lax.axis_index("pcol")
    x, z = prow // NZ, prow % NZ
    root = lambda x, z: x == 0 and z < 3
    where = jnp.stack([prow, pcol, lax.rem(x + 2 * z, 4)]).astype(jnp.int32)
    faces, *cut = pack_first(where, pattern, row_perm, matrix)
    sent = [hop(cut[d], [(d, 0)], root) for d in (2, 1, 3)]
    faces = lax.all_to_all(faces, "pcol", 0, 0)
    columns = to_all(faces[:3])
    extra = jnp.stack(
        [jnp.where(z == 0, faces[1, 0], faces[0, 0]), jnp.where(z == 2, faces[1, 0], faces[2, 0])]
    )
    extra_sent = [hop(extra, [(d, 0)], root) for d in (2, 1, 3)]
    own = jnp.where(x == 0, cut[0], sum(sent))
    own_extra = jnp.where(x == 0, extra, sum(extra_sent))
    own = jnp.concatenate([own, own_extra[:, None]], axis=1)
    far = [
        hop(own[0], [(0, 4)], lambda x, z: z < 3),
        hop(own[1], [(0, 4), (0, 4), (2, 5)], lambda x, z: z < 3),
    ]
    held = [jnp.where(z < 4, own[h], far[h]) for h in range(2)]
    both = jnp.stack(held)
    after = hop(both, [(2, 1)], lambda x, z: z != 3)
    before = hop(both, [(2, -1)], lambda x, z: z != 3)
    two = [
        hop(held[0], [(0, 2)], lambda x, z: z % 4 < 3),
        hop(
            held[1],
            [(0, -2), (0, -2), (0, 2), None, (0, -2), (0, -2), None, (0, -2)],
            lambda x, z: z not in (3, 6),
        ),
    ]

    found = jnp.array(PICK, jnp.int32)[:, :, z].reshape(6)
    mine, half0, half1, corner = merge(found, columns, held[0], held[1], after, before, two[0], two[1])
    corner = lax.all_to_all(corner, "pcol", 0, 0)
    ap0, ap1 = pack(where, pattern, row_perm, matrix, mine)
    lower, higher = hop(mine, [(1, 0)]), hop(mine, [(-1, 0)])
    half0, half1 = hop(half0, [(0, 1)]), hop(half1, [(0, -1)])
    ll, c3, li, raw = left(where, pattern, columns, corner, lower_inv, upper_inv)
    return finish(where, pattern, ap0, ap1, ll, c3, li, raw, mine, lower, higher, half0, half1)


def solution(mesh):
    P = jax.sharding.PartitionSpec
    in_specs = (P(None, "prow", None, "pcol"), P(), P(None, "prow"), P(), P())
    out_specs = P(None, "prow", None, "pcol")
    return jax.shard_map(
        on_device, mesh=mesh, in_specs=in_specs, out_specs=out_specs, check_vma=False
    )
```

time: 737 us -> 176 us (0.24)
  the two profiles are of different devices: /device:TPU:1 before, /device:TPU:64 now
where the time goes in v2:
time: 176 us; the launch traced here: 175 us
  waiting for transfers between devices  65.8 us (37%)
  starting transfers between devices  51.2 us (29%)
  Pallas kernels  38.3 us (22%)
  local copies, waits for them, and re-layouts  16.9 us (10%)
  other arithmetic  1.88 us (1%)
    ppermute x16, waiting for transfers between devices, hop(): return lax.ppermute(array, 'prow', pairs)  52.7 us
    ppermute x16, starting transfers between devices, hop(): return lax.ppermute(array, 'prow', pairs)  37.7 us
    pallas_call x1, Pallas kernels, finish(): pl.pallas_call(finish_body, in_specs=[SMEM, SMEM] + [HERE] * 6 + [ANY] *...  17.1 us
    unnamed x40, local copies, waits for them, and re-layouts  14.8 us
    all_to_all x1, waiting for transfers between devices, on_device(): corner = lax.all_to_all(corner, 'pcol', 0, 0)  10.4 us
    pallas_call x1, Pallas kernels, left(): pl.pallas_call(left_body, in_specs=[SMEM, SMEM, ANY, ANY, ANY, ANY], out_...  7 us
    pallas_call x1, Pallas kernels, pack_first(): pl.pallas_call(pack_first_body, in_specs=[SMEM, SMEM, SMEM, ANY], out_spe...  6.14 us
    all_to_all x1, starting transfers between devices, on_device(): faces = lax.all_to_all(faces, 'pcol', 0, 0)  4.61 us
  transfers between devices with their start and end apart: 19, of which 9 were waited for; matrix products, arithmetic and copies ran while one was open for 2% of the time, Pallas kernels for 6%

profile of v2, /device:TPU:64, one launch (start us, length us, event | category | flops | bytes accessed | tf_op | source)
XLA Modules:
  0.0 174.6 jit_solution(9561948432642119440)
XLA Ops:
  0.7 6.1 %pack_first.1 = (f32[8,2,32,256]{3,2,1,0:T(8,128)}, f32[2,8,32,256]{3,2,1,0:T(8,128)}, f32[2,8,32,256]{3,2,1,0:T(8,128)}, f32[2,8,32,256]{3,2,1,0:T(8,128)}, f32[2,8,32,256]{3,2,1,0:T(8,128)}) custom-call(s32[3]{0:T(128)} %pad_add_fusion.where_ref, s32[64,64]{1,0:T(8,128)} %pattern_ref.7, s32[2,256]{1,0:T(2,128)} %perm_ref.3, f32[2,256,8,256]{3,2,1,0:T(8,128)} %a_ref.3), custom_call_target="tpu_custom_call" | custom-call | tf_op jit(solution)/shard_map/pack_first/pallas_call | solution.py:106
  6.8 4.6 %all-to-all-start = ((f32[8,2,32,256]{3,2,1,0:T(8,128)}), f32[8,2,32,256]{3,2,1,0:T(8,128)S(1)}, u32[]{:S(2)}, u32[]{:S(2)}) async-start(f32[8,2,32,256]{3,2,1,0:T(8,128)} %get-tuple-element.20), calls=%async_computation | async-start | bytes 1048576 | tf_op jit(solution)/shard_map/all_to_all | solution.py:420
  11.4 4.9 %collective-permute-start = (f32[2,8,32,256]{3,2,1,0:T(8,128)}, f32[2,8,32,256]{3,2,1,0:T(8,128)S(1)}, u32[]{:S(2)}, u32[]{:S(2)}) collective-permute-start(f32[2,8,32,256]{3,2,1,0:T(8,128)} %get-tuple-element.22), channel_id=1, source_target_pairs={{0,128},{8,136},{16,144},{1,129},{9,137},{17,145},{2,130},{10,138}... | collective-permute-start | bytes 1572872 | tf_op jit(solution)/shard_map/ppermute | solution.py:397
  19.0 2.7 %all-to-all-done = f32[8,2,32,256]{3,2,1,0:T(8,128)S(1)} async-done(((f32[8,2,32,256]{3,2,1,0:T(8,128)}), f32[8,2,32,256]{3,2,1,0:T(8,128)S(1)}, u32[]{:S(2)}, u32[]{:S(2)}) %all-to-all-start) | async-done | bytes 524320 | tf_op jit(solution)/shard_map/all_to_all | solution.py:420
  21.8 4.7 %collective-permute-start.5 = (f32[2,32,256]{2,1,0:T(8,128)S(1)}, f32[2,32,256]{2,1,0:T(8,128)S(1)}, u32[]{:S(2)}, u32[]{:S(2)}) collective-permute-start(f32[2,32,256]{2,1,0:T(8,128)S(1)} %pad_maximum_fusion.2), channel_id=1, source_target_pairs={{0,192},{8,200},{16,208},{1,193},{9,201},{17,209},{2,194},{10,202}... | collective-permute-start | bytes 196616 | tf_op jit(solution)/shard_map/ppermute | solution.py:397
  27.8 4.7 %collective-permute-done.5 = f32[2,32,256]{2,1,0:T(8,128)S(1)} collective-permute-done((f32[2,32,256]{2,1,0:T(8,128)S(1)}, f32[2,32,256]{2,1,0:T(8,128)S(1)}, u32[]{:S(2)}, u32[]{:S(2)}) %collective-permute-start.5) | collective-permute-done | bytes 65568 | tf_op jit(solution)/shard_map/ppermute | solution.py:397
  33.8 7.7 %collective-permute-done.4 = f32[2,32,256]{2,1,0:T(8,128)S(1)} collective-permute-done((f32[2,32,256]{2,1,0:T(8,128)S(1)}, f32[2,32,256]{2,1,0:T(8,128)S(1)}, u32[]{:S(2)}, u32[]{:S(2)}) %collective-permute-start.4) | collective-permute-done | bytes 65568 | tf_op jit(solution)/shard_map/ppermute | solution.py:397
  45.4 4.4 %all-to-all-start.1 = ((f32[8,3,2,32,256]{4,3,2,1,0:T(8,128)}), f32[8,3,2,32,256]{4,3,2,1,0:T(8,128)S(1)}, u32[]{:S(2)}, u32[]{:S(2)}) async-start(f32[8,3,2,32,256]{4,3,2,1,0:T(8,128)} %broadcast_in_dim.6), calls=%async_computation.1 | async-start | bytes 3145728 | tf_op jit(solution)/shard_map/all_to_all | solution.py:402
  51.2 12.5 %collective-permute-done.6 = f32[9,32,256]{2,1,0:T(8,128)S(1)} collective-permute-done((f32[9,32,256]{2,1,0:T(8,128)S(1)}, f32[9,32,256]{2,1,0:T(8,128)S(1)}, u32[]{:S(2)}, u32[]{:S(2)}) %collective-permute-start.6) | collective-permute-done | bytes 294944 | tf_op jit(solution)/shard_map/ppermute | solution.py:397
  64.7 4.8 %collective-permute-start.9 = (f32[2,9,32,256]{3,2,1,0:T(8,128)}, f32[2,9,32,256]{3,2,1,0:T(8,128)S(1)}, u32[]{:S(2)}, u32[]{:S(2)}) collective-permute-start(f32[2,9,32,256]{3,2,1,0:T(8,128)} %pad_maximum_fusion), channel_id=1, source_target_pairs={{0,184},{8,128},{16,136},{32,152},{40,160},{48,168},{56,176},{64,2... | collective-permute-start | bytes 1769480 | tf_op jit(solution)/shard_map/ppermute | solution.py:397
  69.6 1.9 %collective-permute-start.8 = (f32[2,9,32,256]{3,2,1,0:T(8,128)}, f32[2,9,32,256]{3,2,1,0:T(8,128)S(1)}, u32[]{:S(2)}, u32[]{:S(2)}) collective-permute-start(f32[2,9,32,256]{3,2,1,0:T(8,128)} %pad_maximum_fusion), channel_id=1, source_target_pairs={{0,136},{8,144},{16,152},{32,168},{40,176},{48,184},{56,128},{64,2... | collective-permute-start | bytes 1769480 | tf_op jit(solution)/shard_map/ppermute | solution.py:397
  71.5 7.5 %collective-permute-start.11 = (f32[9,32,256]{2,1,0:T(8,128)S(1)}, f32[9,32,256]{2,1,0:T(8,128)}, u32[]{:S(2)}, u32[]{:S(2)}) collective-permute-start(f32[9,32,256]{2,1,0:T(8,128)S(1)} %broadcast_select_fusion.held1), channel_id=1, source_target_pairs={{0,48},{8,56},{16,32},{32,16},{40,24},{56,40},{64,112},{72,120},{8... | collective-permute-start | bytes 884744 | tf_op jit(solution)/shard_map/ppermute | solution.py:397
  78.9 1.9 %collective-permute-start.10 = (f32[9,32,256]{2,1,0:T(8,128)S(1)}, f32[9,32,256]{2,1,0:T(8,128)}, u32[]{:S(2)}, u32[]{:S(2)}) collective-permute-start(f32[9,32,256]{2,1,0:T(8,128)S(1)} %broadcast_select_fusion.1.held0), channel_id=1, source_target_pairs={{0,16},{8,24},{16,32},{32,48},{40,56},{48,0},{64,80},{72,88},{80,9... | collective-permute-start | bytes 884744 | tf_op jit(solution)/shard_map/ppermute | solution.py:397
  81.7 21.6 %collective-permute-done.11.two1 = f32[9,32,256]{2,1,0:T(8,128)} collective-permute-done((f32[9,32,256]{2,1,0:T(8,128)S(1)}, f32[9,32,256]{2,1,0:T(8,128)}, u32[]{:S(2)}, u32[]{:S(2)}) %collective-permute-start.11) | collective-permute-done | bytes 294944 | tf_op jit(solution)/shard_map/ppermute | solution.py:397
  103.3 4.8 %collective-permute-done.10.two0 = f32[9,32,256]{2,1,0:T(8,128)} collective-permute-done((f32[9,32,256]{2,1,0:T(8,128)S(1)}, f32[9,32,256]{2,1,0:T(8,128)}, u32[]{:S(2)}, u32[]{:S(2)}) %collective-permute-start.10) | collective-permute-done | bytes 294944 | tf_op jit(solution)/shard_map/ppermute | solution.py:397
  112.9 3.8 %merge.1 = (f32[2,3,8,32,256]{4,3,2,1,0:T(8,128)S(1)}, f32[3,8,32,256]{3,2,1,0:T(8,128)S(1)}, f32[3,8,32,256]{3,2,1,0:T(8,128)S(1)}, f32[8,3,2,32,256]{4,3,2,1,0:T(8,128)S(1)}) custom-call(s32[6]{0:T(128)S(1)} %reshape_squeeze.3.found_ref, f32[8,3,2,32,256]{4,3,2,1,0:T(8,128)S(1)} %all-to-all-done.1.columns_ref, f32[9,32,256]{2,1,0:T(8,128)S(1)} %copy-done.2, ...), custom_call_target="tpu_custom_call" | custom-call | tf_op jit(solution)/shard_map/merge/pallas_call | solution.py:184
  119.6 2.0 %collective-permute-start.12 = (f32[2,3,8,32,256]{4,3,2,1,0:T(8,128)S(1)}, f32[2,3,8,32,256]{4,3,2,1,0:T(8,128)}, u32[]{:S(2)}, u32[]{:S(2)}) collective-permute-start(f32[2,3,8,32,256]{4,3,2,1,0:T(8,128)S(1)} %get-tuple-element.25.after_ref.mine), channel_id=1, source_target_pairs={{0,64},{8,72},{16,80},{24,88},{32,96},{40,104},{48,112},{56,120},{... | collective-permute-start | bytes 4718600 | tf_op jit(solution)/shard_map/ppermute | solution.py:397
  121.7 4.4 %all-to-all-start.2 = ((f32[8,3,2,32,256]{4,3,2,1,0:T(8,128)}), f32[8,3,2,32,256]{4,3,2,1,0:T(8,128)}, u32[]{:S(2)}, u32[]{:S(2)}) async-start(f32[8,3,2,32,256]{4,3,2,1,0:T(8,128)} %copy-done.7), calls=%async_computation.2 | async-start | bytes 3145728 | tf_op jit(solution)/shard_map/all_to_all | solution.py:448
  126.2 2.0 %collective-permute-start.15 = (f32[3,8,32,256]{3,2,1,0:T(8,128)}, f32[3,8,32,256]{3,2,1,0:T(8,128)}, u32[]{:S(2)}, u32[]{:S(2)}) collective-permute-start(f32[3,8,32,256]{3,2,1,0:T(8,128)} %copy-done.17), channel_id=1, source_target_pairs={{0,56},{8,0},{16,8},{24,16},{32,24},{40,32},{48,40},{56,48},{64,12... | collective-permute-start | bytes 2359304 | tf_op jit(solution)/shard_map/ppermute | solution.py:397
  128.2 2.2 %copy-done = f32[2,256,8,256]{3,2,1,0:T(8,128)S(1)} copy-done((f32[2,256,8,256]{3,2,1,0:T(8,128)S(1)}, f32[2,256,8,256]{3,2,1,0:T(8,128)}, u32[]{:S(2)}) %copy-start) | copy-done | bytes 4194328
  130.4 4.2 %pack.1 = (f32[8,256,256]{2,1,0:T(8,128)S(1)}, f32[8,256,256]{2,1,0:T(8,128)S(1)}) custom-call(s32[3]{0:T(128)S(1)} %copy-done.15, s32[64,64]{1,0:T(8,128)S(1)} %copy-done.14, s32[2,256]{1,0:T(2,128)S(1)} %copy-done.16, f32[2,256,8,256]{3,2,1,0:T(8,128)S(1)} %copy-done, f32[2,3,8,32,256]{4,3,2,1,0:T(8,128)S(1)} %get-tuple-element.25.after_ref.mine), custom_call_target="tpu_custom_call" | custom-call | tf_op jit(solution)/shard_map/pack/pallas_call | solution.py:130
  137.3 10.4 %all-to-all-done.2.corner_ref = f32[8,3,2,32,256]{4,3,2,1,0:T(8,128)} async-done(((f32[8,3,2,32,256]{4,3,2,1,0:T(8,128)}), f32[8,3,2,32,256]{4,3,2,1,0:T(8,128)}, u32[]{:S(2)}, u32[]{:S(2)}) %all-to-all-start.2) | async-done | bytes 1572896 | tf_op jit(solution)/shard_map/all_to_all | solution.py:448
  149.9 7.0 %left.1 = (bf16[512,2304]{1,0:T(8,128)(2,1)S(1)}, bf16[3,256,768]{2,1,0:T(8,128)(2,1)S(1)}, bf16[3,256,768]{2,1,0:T(8,128)(2,1)S(1)}, f32[3,2,256,256]{3,2,1,0:T(8,128)S(1)}) custom-call(s32[3]{0:T(128)S(1)} %copy-done.15, s32[64,64]{1,0:T(8,128)S(1)} %copy-done.14, f32[8,3,2,32,256]{4,3,2,1,0:T(8,128)S(1)} %all-to-all-done.1.columns_ref, ...), custom_call_target="tpu_custom_call" | custom-call | tf_op jit(solution)/shard_map/left/pallas_call | solution.py:256
  157.3 17.1 %finish.1 = f32[2,256,8,256]{3,2,1,0:T(8,128)} custom-call(s32[3]{0:T(128)S(1)} %copy-done.15, s32[64,64]{1,0:T(8,128)S(1)} %copy-done.14, f32[8,256,256]{2,1,0:T(8,128)S(1)} %copy-done.4, f32[8,256,256]{2,1,0:T(8,128)S(1)} %copy-done.6, bf16[512,2304]{1,0:T(8,128)(2,1)S(1)} %get-tuple-element.29.ll, bf16[3,256,768]{2,1,0:T(8,128)(2,1)S(1)} %get-tuple-element.30.c3, ...), custom_call_target="tpu_custom_call" | custom-call | tf_op jit(solution)/shard_map/finish/pallas_call | solution.py:373
  (72 shorter events, 25.9 us)
Async XLA Ops:
  6.8 35.7 %copy-start.19 = (f32[2,8,32,256]{3,2,1,0:T(8,128)S(1)}, f32[2,8,32,256]{3,2,1,0:T(8,128)}, u32[]{:S(2)}) copy-start(f32[2,8,32,256]{3,2,1,0:T(8,128)} %get-tuple-element.21) | copy-start | bytes 1572868
  6.8 15.0 %all-to-all-start = ((f32[8,2,32,256]{3,2,1,0:T(8,128)}), f32[8,2,32,256]{3,2,1,0:T(8,128)S(1)}, u32[]{:S(2)}, u32[]{:S(2)}) async-start(f32[8,2,32,256]{3,2,1,0:T(8,128)} %get-tuple-element.20), calls=%async_computation | async-start | bytes 1048576 | tf_op jit(solution)/shard_map/all_to_all | solution.py:420
  11.4 31.0 %collective-permute-start = (f32[2,8,32,256]{3,2,1,0:T(8,128)}, f32[2,8,32,256]{3,2,1,0:T(8,128)S(1)}, u32[]{:S(2)}, u32[]{:S(2)}) collective-permute-start(f32[2,8,32,256]{3,2,1,0:T(8,128)} %get-tuple-element.22), channel_id=1, source_target_pairs={{0,128},{8,136},{16,144},{1,129},{9,137},{17,145},{2,130},{10,138}... | collective-permute-start | bytes 1572872 | tf_op jit(solution)/shard_map/ppermute | solution.py:397
  16.4 26.1 %collective-permute-start.1 = (f32[2,8,32,256]{3,2,1,0:T(8,128)}, f32[2,8,32,256]{3,2,1,0:T(8,128)S(1)}, u32[]{:S(2)}, u32[]{:S(2)}) collective-permute-start(f32[2,8,32,256]{3,2,1,0:T(8,128)} %get-tuple-element.23), channel_id=1, source_target_pairs={{0,64},{8,72},{16,80},{1,65},{9,73},{17,81},{2,66},{10,74},{18,82}... | collective-permute-start | bytes 1572872 | tf_op jit(solution)/shard_map/ppermute | solution.py:397
  17.7 24.8 %collective-permute-start.2 = (f32[2,8,32,256]{3,2,1,0:T(8,128)}, f32[2,8,32,256]{3,2,1,0:T(8,128)S(1)}, u32[]{:S(2)}, u32[]{:S(2)}) collective-permute-start(f32[2,8,32,256]{3,2,1,0:T(8,128)} %get-tuple-element.24), channel_id=1, source_target_pairs={{0,192},{8,200},{16,208},{1,193},{9,201},{17,209},{2,194},{10,202}... | collective-permute-start | bytes 1572872 | tf_op jit(solution)/shard_map/ppermute | solution.py:397
  21.8 10.7 %collective-permute-start.5 = (f32[2,32,256]{2,1,0:T(8,128)S(1)}, f32[2,32,256]{2,1,0:T(8,128)S(1)}, u32[]{:S(2)}, u32[]{:S(2)}) collective-permute-start(f32[2,32,256]{2,1,0:T(8,128)S(1)} %pad_maximum_fusion.2), channel_id=1, source_target_pairs={{0,192},{8,200},{16,208},{1,193},{9,201},{17,209},{2,194},{10,202}... | collective-permute-start | bytes 196616 | tf_op jit(solution)/shard_map/ppermute | solution.py:397
  26.5 14.9 %collective-permute-start.4 = (f32[2,32,256]{2,1,0:T(8,128)S(1)}, f32[2,32,256]{2,1,0:T(8,128)S(1)}, u32[]{:S(2)}, u32[]{:S(2)}) collective-permute-start(f32[2,32,256]{2,1,0:T(8,128)S(1)} %pad_maximum_fusion.2), channel_id=1, source_target_pairs={{0,64},{8,72},{16,80},{1,65},{9,73},{17,81},{2,66},{10,74},{18,82}... | collective-permute-start | bytes 196616 | tf_op jit(solution)/shard_map/ppermute | solution.py:397
  32.5 10.0 %collective-permute-start.3 = (f32[2,32,256]{2,1,0:T(8,128)S(1)}, f32[2,32,256]{2,1,0:T(8,128)S(1)}, u32[]{:S(2)}, u32[]{:S(2)}) collective-permute-start(f32[2,32,256]{2,1,0:T(8,128)S(1)} %pad_maximum_fusion.2), channel_id=1, source_target_pairs={{0,128},{8,136},{16,144},{1,129},{9,137},{17,145},{2,130},{10,138}... | collective-permute-start | bytes 196616 | tf_op jit(solution)/shard_map/ppermute | solution.py:397
  42.7 8.4 %collective-permute-start.7 = (f32[9,32,256]{2,1,0:T(8,128)S(1)}, f32[9,32,256]{2,1,0:T(8,128)S(1)}, u32[]{:S(2)}, u32[]{:S(2)}) collective-permute-start(f32[9,32,256]{2,1,0:T(8,128)S(1)} %get-tuple-element.35), channel_id=1, source_target_pairs={{0,32},{8,40},{16,184},{64,96},{72,104},{80,248},{128,160},{136,16... | collective-permute-start | bytes 884744 | tf_op jit(solution)/shard_map/ppermute | solution.py:397
  45.4 64.4 %all-to-all-start.1 = ((f32[8,3,2,32,256]{4,3,2,1,0:T(8,128)}), f32[8,3,2,32,256]{4,3,2,1,0:T(8,128)S(1)}, u32[]{:S(2)}, u32[]{:S(2)}) async-start(f32[8,3,2,32,256]{4,3,2,1,0:T(8,128)} %broadcast_in_dim.6), calls=%async_computation.1 | async-start | bytes 3145728 | tf_op jit(solution)/shard_map/all_to_all | solution.py:402
  49.8 13.9 %collective-permute-start.6 = (f32[9,32,256]{2,1,0:T(8,128)S(1)}, f32[9,32,256]{2,1,0:T(8,128)S(1)}, u32[]{:S(2)}, u32[]{:S(2)}) collective-permute-start(f32[9,32,256]{2,1,0:T(8,128)S(1)} %get-tuple-element.36), channel_id=1, source_target_pairs={{0,32},{8,40},{16,48},{64,96},{72,104},{80,112},{128,160},{136,168... | collective-permute-start | bytes 884744 | tf_op jit(solution)/shard_map/ppermute | solution.py:397
  63.8 45.2 %copy-start.1 = (f32[9,32,256]{2,1,0:T(8,128)}, f32[9,32,256]{2,1,0:T(8,128)S(1)}, u32[]{:S(2)}) copy-start(f32[9,32,256]{2,1,0:T(8,128)S(1)} %broadcast_select_fusion.1.held0) | copy-start | bytes 884740
  64.7 43.4 %collective-permute-start.9 = (f32[2,9,32,256]{3,2,1,0:T(8,128)}, f32[2,9,32,256]{3,2,1,0:T(8,128)S(1)}, u32[]{:S(2)}, u32[]{:S(2)}) collective-permute-start(f32[2,9,32,256]{3,2,1,0:T(8,128)} %pad_maximum_fusion), channel_id=1, source_target_pairs={{0,184},{8,128},{16,136},{32,152},{40,160},{48,168},{56,176},{64,2... | collective-permute-start | bytes 1769480 | tf_op jit(solution)/shard_map/ppermute | solution.py:397
  69.6 39.4 %collective-permute-start.8 = (f32[2,9,32,256]{3,2,1,0:T(8,128)}, f32[2,9,32,256]{3,2,1,0:T(8,128)S(1)}, u32[]{:S(2)}, u32[]{:S(2)}) collective-permute-start(f32[2,9,32,256]{3,2,1,0:T(8,128)} %pad_maximum_fusion), channel_id=1, source_target_pairs={{0,136},{8,144},{16,152},{32,168},{40,176},{48,184},{56,128},{64,2... | collective-permute-start | bytes 1769480 | tf_op jit(solution)/shard_map/ppermute | solution.py:397
  71.5 31.8 %collective-permute-start.11 = (f32[9,32,256]{2,1,0:T(8,128)S(1)}, f32[9,32,256]{2,1,0:T(8,128)}, u32[]{:S(2)}, u32[]{:S(2)}) collective-permute-start(f32[9,32,256]{2,1,0:T(8,128)S(1)} %broadcast_select_fusion.held1), channel_id=1, source_target_pairs={{0,48},{8,56},{16,32},{32,16},{40,24},{56,40},{64,112},{72,120},{8... | collective-permute-start | bytes 884744 | tf_op jit(solution)/shard_map/ppermute | solution.py:397
  78.9 29.2 %collective-permute-start.10 = (f32[9,32,256]{2,1,0:T(8,128)S(1)}, f32[9,32,256]{2,1,0:T(8,128)}, u32[]{:S(2)}, u32[]{:S(2)}) collective-permute-start(f32[9,32,256]{2,1,0:T(8,128)S(1)} %broadcast_select_fusion.1.held0), channel_id=1, source_target_pairs={{0,16},{8,24},{16,32},{32,48},{40,56},{48,0},{64,80},{72,88},{80,9... | collective-permute-start | bytes 884744 | tf_op jit(solution)/shard_map/ppermute | solution.py:397
  119.6 37.3 %collective-permute-start.13 = (f32[2,3,8,32,256]{4,3,2,1,0:T(8,128)S(1)}, f32[2,3,8,32,256]{4,3,2,1,0:T(8,128)}, u32[]{:S(2)}, u32[]{:S(2)}) collective-permute-start(f32[2,3,8,32,256]{4,3,2,1,0:T(8,128)S(1)} %get-tuple-element.25.after_ref.mine), channel_id=1, source_target_pairs={{0,192},{8,200},{16,208},{24,216},{32,224},{40,232},{48,240},{56,2... | collective-permute-start | bytes 4718600 | tf_op jit(solution)/shard_map/ppermute | solution.py:397
  119.6 37.7 %collective-permute-start.12 = (f32[2,3,8,32,256]{4,3,2,1,0:T(8,128)S(1)}, f32[2,3,8,32,256]{4,3,2,1,0:T(8,128)}, u32[]{:S(2)}, u32[]{:S(2)}) collective-permute-start(f32[2,3,8,32,256]{4,3,2,1,0:T(8,128)S(1)} %get-tuple-element.25.after_ref.mine), channel_id=1, source_target_pairs={{0,64},{8,72},{16,80},{24,88},{32,96},{40,104},{48,112},{56,120},{... | collective-permute-start | bytes 4718600 | tf_op jit(solution)/shard_map/ppermute | solution.py:397
  121.7 6.5 %copy-start.16 = (s32[2,256]{1,0:T(2,128)S(1)}, s32[2,256]{1,0:T(2,128)}, u32[]{:S(2)}) copy-start(s32[2,256]{1,0:T(2,128)} %perm_ref.3) | copy-start | bytes 6148
  121.7 26.0 %all-to-all-start.2 = ((f32[8,3,2,32,256]{4,3,2,1,0:T(8,128)}), f32[8,3,2,32,256]{4,3,2,1,0:T(8,128)}, u32[]{:S(2)}, u32[]{:S(2)}) async-start(f32[8,3,2,32,256]{4,3,2,1,0:T(8,128)} %copy-done.7), calls=%async_computation.2 | async-start | bytes 3145728 | tf_op jit(solution)/shard_map/all_to_all | solution.py:448
  126.1 30.9 %collective-permute-start.14 = (f32[3,8,32,256]{3,2,1,0:T(8,128)}, f32[3,8,32,256]{3,2,1,0:T(8,128)}, u32[]{:S(2)}, u32[]{:S(2)}) collective-permute-start(f32[3,8,32,256]{3,2,1,0:T(8,128)} %copy-done.18), channel_id=1, source_target_pairs={{0,8},{8,16},{16,24},{24,32},{32,40},{40,48},{48,56},{56,0},{64,72... | collective-permute-start | bytes 2359304 | tf_op jit(solution)/shard_map/ppermute | solution.py:397
  126.2 30.8 %collective-permute-start.15 = (f32[3,8,32,256]{3,2,1,0:T(8,128)}, f32[3,8,32,256]{3,2,1,0:T(8,128)}, u32[]{:S(2)}, u32[]{:S(2)}) collective-permute-start(f32[3,8,32,256]{3,2,1,0:T(8,128)} %copy-done.17), channel_id=1, source_target_pairs={{0,56},{8,0},{16,8},{24,16},{32,24},{40,32},{48,40},{56,48},{64,12... | collective-permute-start | bytes 2359304 | tf_op jit(solution)/shard_map/ppermute | solution.py:397
  149.9 7.4 %copy-start.4 = (f32[8,256,256]{2,1,0:T(8,128)S(1)}, f32[8,256,256]{2,1,0:T(8,128)}, u32[]{:S(2)}) copy-start(f32[8,256,256]{2,1,0:T(8,128)} %copy-done.3) | copy-start | bytes 6291460
  149.9 7.4 %copy-start.6 = (f32[8,256,256]{2,1,0:T(8,128)S(1)}, f32[8,256,256]{2,1,0:T(8,128)}, u32[]{:S(2)}) copy-start(f32[8,256,256]{2,1,0:T(8,128)} %copy-done.5) | copy-start | bytes 6291460
  (15 other events, 27.9 us)

commit v3 on v2

--- a/solution.py
+++ b/solution.py
@@ -138,60 +138,94 @@
     )(where, pattern, perm, matrix, after)
 
 
+def hold_body(where_ref, own_ref, far0, far1, columns_ref, both_ref, sem):
+    near = where_ref[3] < 4
+    for h, far in enumerate((far0, far1)):
+        here = pltpu.make_async_copy(own_ref.at[h], both_ref.at[h], sem.at[h])
+        there = pltpu.make_async_copy(far, both_ref.at[h], sem.at[h])
+
+        @pl.when(near)
+        def _():
+            here.start()
+
+        @pl.when(jnp.logical_not(near))
+        def _():
+            there.start()
+
+    for h in range(2):
+        pltpu.make_async_copy(own_ref.at[h], both_ref.at[h], sem.at[h]).wait()
+
+
+def hold(where, own, far, columns):
+    return pl.pallas_call(
+        hold_body,
+        in_specs=[SMEM] + [HERE] * 3 + [ANY],
+        out_specs=HERE,
+        out_shape=shaped((2, 9, 32, 256), F32),
+        scratch_shapes=[pltpu.SemaphoreType.DMA((2,))],
+        compiler_params=params(4),
+        name="hold",
+    )(where, own, far[0], far[1], columns)
+
+
 def merge_body(
-    found_ref, columns_ref, held0, held1, after, before, two0, two1,
-    all_ref, half0, half1, corner_ref, slices, sem,
+    found_ref, held, after, before, two,
+    all_ref, half0, half1, corner_ref, stage, slices, sem,
 ):
+    pieces = [(r, h) for r in range(3) for h in range(2)]
+    arrive = []
+    for n, (r, h) in enumerate(pieces):
+        found = found_ref[n]
+
+        def load(part, n=n, r=r, h=h):
+            return pltpu.make_async_copy(part.at[h], stage.at[h, r], sem.at[n])
+
+        for which, part in enumerate((held, after, before, two)):
+
+            @pl.when(found == which)
+            def _():
+                load(part).start()
+
+        arrive.append(load(held))
     eight = pl.ds(0, 8)
-    waits = []
-    for r in range(3):
-        for h in range(2):
-            n = (r * 2 + h) * 3
-            found = found_ref[r * 2 + h]
-            sources = ((held0, held1)[h], after.at[h], before.at[h], (two0, two1)[h])
-
-            def copies(source, n=n, r=r, h=h):
-                return [
-                    pltpu.make_async_copy(source.at[8], slices.at[r, h], sem.at[n]),
-                    pltpu.make_async_copy(source.at[eight], all_ref.at[h, r], sem.at[n + 1]),
-                    pltpu.make_async_copy(source.at[eight], (half0, half1)[h].at[r], sem.at[n + 2]),
-                ]
-
-            for which, source in enumerate(sources):
-
-                @pl.when(found == which)
-                def _():
-                    for one in copies(source):
-                        one.start()
-
-            waits.append(copies(sources[0]))
-    for group in waits:
-        group[0].wait()
-    last = [
-        pltpu.make_async_copy(slices, corner_ref.at[q], sem.at[18 + q]) for q in range(8)
-    ]
-    for one in last:
-        one.start()
-    for group in waits:
-        group[1].wait()
-        group[2].wait()
+    small, last = [], []
+    for n, (r, h) in enumerate(pieces):
+        arrive[n].wait()
+        k = 6 + 3 * n
+        last.append(pltpu.make_async_copy(stage.at[h, r, eight], all_ref.at[h, r], sem.at[k]))
+        last.append(
+            pltpu.make_async_copy(stage.at[h, r, eight], (half0, half1)[h].at[r], sem.at[k + 1])
+        )
+        small.append(pltpu.make_async_copy(stage.at[h, r, 8], slices.at[r, h], sem.at[k + 2]))
+        last[-2].start()
+        last[-1].start()
+        small[-1].start()
+    for one in small:
+        one.wait()
+    for q in range(8):
+        last.append(pltpu.make_async_copy(slices, corner_ref.at[q], sem.at[24 + q]))
+        last[-1].start()
     for one in last:
         one.wait()
 
 
-def merge(found, columns, *parts):
+def merge(found, *parts):
     half = shaped((3, 8, 32, 256), F32)
     return pl.pallas_call(
         merge_body,
-        in_specs=[SMEM] + [ANY] * 7,
+        in_specs=[SMEM] + [ANY] * 4,
         out_specs=[ANY] * 4,
         out_shape=[
             shaped((2, 3, 8, 32, 256), F32), half, half, shaped((8, 3, 2, 32, 256), F32)
         ],
-        scratch_shapes=[VMEM((3, 2, 32, 256), F32), pltpu.SemaphoreType.DMA((26,))],
-        compiler_params=params(8),
+        scratch_shapes=[
+            VMEM((2, 3, 9, 32, 256), F32),
+            VMEM((3, 2, 32, 256), F32),
+            pltpu.SemaphoreType.DMA((32,)),
+        ],
+        compiler_params=params(58),
         name="merge",
-    )(found, columns, *parts)
+    )(found, *parts)
 
 
 def left_body(
@@ -381,7 +415,7 @@
             VMEM((2, 256, 8, 256), F32),
             pltpu.SemaphoreType.DMA((48,)),
         ],
-        compiler_params=params(32),
+        compiler_params=params(28),
         name="finish",
     )(where, pattern, ap0, ap1, ll, c3, li, raw, *mains)
 
@@ -414,7 +448,7 @@
     pcol = lax.axis_index("pcol")
     x, z = prow // NZ, prow % NZ
     root = lambda x, z: x == 0 and z < 3
-    where = jnp.stack([prow, pcol, lax.rem(x + 2 * z, 4)]).astype(jnp.int32)
+    where = jnp.stack([prow, pcol, lax.rem(x + 2 * z, 4), z]).astype(jnp.int32)
     faces, *cut = pack_first(where, pattern, row_perm, matrix)
     sent = [hop(cut[d], [(d, 0)], root) for d in (2, 1, 3)]
     faces = lax.all_to_all(faces, "pcol", 0, 0)
@@ -430,21 +464,13 @@
         hop(own[0], [(0, 4)], lambda x, z: z < 3),
         hop(own[1], [(0, 4), (0, 4), (2, 5)], lambda x, z: z < 3),
     ]
-    held = [jnp.where(z < 4, own[h], far[h]) for h in range(2)]
-    both = jnp.stack(held)
+    both = hold(where, own, far, columns)
     after = hop(both, [(2, 1)], lambda x, z: z != 3)
     before = hop(both, [(2, -1)], lambda x, z: z != 3)
-    two = [
-        hop(held[0], [(0, 2)], lambda x, z: z % 4 < 3),
-        hop(
-            held[1],
-            [(0, -2), (0, -2), (0, 2), None, (0, -2), (0, -2), None, (0, -2)],
-            lambda x, z: z not in (3, 6),
-        ),
-    ]
-
+    steps = [(0, 2), (0, -2), (0, 2), None, (0, 2), (0, -2), (0, 2), (0, -2)]
+    two = hop(both, steps, lambda x, z: z != 3)
     found = jnp.array(PICK, jnp.int32)[:, :, z].reshape(6)
-    mine, half0, half1, corner = merge(found, columns, held[0], held[1], after, before, two[0], two[1])
+    mine, half0, half1, corner = merge(found, both, after, before, two)
     corner = lax.all_to_all(corner, "pcol", 0, 0)
     ap0, ap1 = pack(where, pattern, row_perm, matrix, mine)
     lower, higher = hop(mine, [(1, 0)]), hop(mine, [(-1, 0)])

time: 176 us -> 170 us (0.966)
  the two profiles are of different devices: /device:TPU:64 before, /device:TPU:1 now
where the time goes in v3:
time: 170 us; the launch traced here: 169 us
  starting transfers between devices  60.2 us (35%)
  waiting for transfers between devices  57.1 us (34%)
  Pallas kernels  39.2 us (23%)
  local copies, waits for them, and re-layouts  9.85 us (6%)
  other arithmetic  2.06 us (1%)
    ppermute x15, waiting for transfers between devices, hop(): return lax.ppermute(array, 'prow', pairs)  46.8 us
    ppermute x15, starting transfers between devices, hop(): return lax.ppermute(array, 'prow', pairs)  43.7 us
    pallas_call x1, Pallas kernels, finish(): pl.pallas_call(finish_body, in_specs=[SMEM, SMEM] + [HERE] * 6 + [ANY] *...  17.1 us
    all_to_all x1, waiting for transfers between devices, on_device(): corner = lax.all_to_all(corner, 'pcol', 0, 0)  9.03 us
    unnamed x30, local copies, waits for them, and re-layouts  7.16 us
    pallas_call x1, Pallas kernels, left(): pl.pallas_call(left_body, in_specs=[SMEM, SMEM, ANY, ANY, ANY, ANY], out_...  7.01 us
    all_to_all x1, starting transfers between devices, on_device(): faces = lax.all_to_all(faces, 'pcol', 0, 0)  6.65 us
    pallas_call x1, Pallas kernels, pack_first(): pl.pallas_call(pack_first_body, in_specs=[SMEM, SMEM, SMEM, ANY], out_spe...  6.14 us
  transfers between devices with their start and end apart: 18, of which 9 were waited for; matrix products, arithmetic and copies ran while one was open for 2% of the time, Pallas kernels for 7%

profile of v3, /device:TPU:1, one launch (start us, length us, event | category | flops | bytes accessed | tf_op | source)
XLA Modules:
  0.0 168.9 jit_solution(18074391599723999476)
XLA Ops:
  0.6 6.1 %pack_first.1 = (f32[8,2,32,256]{3,2,1,0:T(8,128)}, f32[2,8,32,256]{3,2,1,0:T(8,128)}, f32[2,8,32,256]{3,2,1,0:T(8,128)}, f32[2,8,32,256]{3,2,1,0:T(8,128)}, f32[2,8,32,256]{3,2,1,0:T(8,128)}) custom-call(s32[4]{0:T(128)} %pad_add_fusion.where_ref, s32[64,64]{1,0:T(8,128)} %pattern_ref.7, s32[2,256]{1,0:T(2,128)} %perm_ref.3, f32[2,256,8,256]{3,2,1,0:T(8,128)} %a_ref.3), custom_call_target="tpu_custom_call" | custom-call | tf_op jit(solution)/shard_map/pack_first/pallas_call | solution.py:106
  6.7 6.6 %all-to-all-start = ((f32[8,2,32,256]{3,2,1,0:T(8,128)}), f32[8,2,32,256]{3,2,1,0:T(8,128)S(1)}, u32[]{:S(2)}, u32[]{:S(2)}) async-start(f32[8,2,32,256]{3,2,1,0:T(8,128)} %get-tuple-element.24), calls=%async_computation | async-start | bytes 1048576 | tf_op jit(solution)/shard_map/all_to_all | solution.py:454
  13.4 4.0 %collective-permute-start = (f32[2,8,32,256]{3,2,1,0:T(8,128)}, f32[2,8,32,256]{3,2,1,0:T(8,128)S(1)}, u32[]{:S(2)}, u32[]{:S(2)}) collective-permute-start(f32[2,8,32,256]{3,2,1,0:T(8,128)} %get-tuple-element.21), channel_id=1, source_target_pairs={{0,128},{8,136},{16,144},{1,129},{9,137},{17,145},{2,130},{10,138}... | collective-permute-start | bytes 1572872 | tf_op jit(solution)/shard_map/ppermute | solution.py:431
  17.4 2.1 %collective-permute-start.1 = (f32[2,8,32,256]{3,2,1,0:T(8,128)}, f32[2,8,32,256]{3,2,1,0:T(8,128)}, u32[]{:S(2)}, u32[]{:S(2)}) collective-permute-start(f32[2,8,32,256]{3,2,1,0:T(8,128)} %get-tuple-element.22), channel_id=1, source_target_pairs={{0,64},{8,72},{16,80},{1,65},{9,73},{17,81},{2,66},{10,74},{18,82}... | collective-permute-start | bytes 1572872 | tf_op jit(solution)/shard_map/ppermute | solution.py:431
  19.5 2.1 %collective-permute-start.2 = (f32[2,8,32,256]{3,2,1,0:T(8,128)}, f32[2,8,32,256]{3,2,1,0:T(8,128)}, u32[]{:S(2)}, u32[]{:S(2)}) collective-permute-start(f32[2,8,32,256]{3,2,1,0:T(8,128)} %get-tuple-element.23), channel_id=1, source_target_pairs={{0,192},{8,200},{16,208},{1,193},{9,201},{17,209},{2,194},{10,202}... | collective-permute-start | bytes 1572872 | tf_op jit(solution)/shard_map/ppermute | solution.py:431
  24.2 4.5 %all-to-all-start.1 = ((f32[8,3,2,32,256]{4,3,2,1,0:T(8,128)}), f32[8,3,2,32,256]{4,3,2,1,0:T(8,128)S(1)}, u32[]{:S(2)}, u32[]{:S(2)}) async-start(f32[8,3,2,32,256]{4,3,2,1,0:T(8,128)} %broadcast_in_dim.7), calls=%async_computation.1 | async-start | bytes 3145728 | tf_op jit(solution)/shard_map/all_to_all | solution.py:436
  28.8 3.7 %collective-permute-start.5 = (f32[2,32,256]{2,1,0:T(8,128)S(1)}, f32[2,32,256]{2,1,0:T(8,128)S(1)}, u32[]{:S(2)}, u32[]{:S(2)}) collective-permute-start(f32[2,32,256]{2,1,0:T(8,128)S(1)} %pad_maximum_fusion.1), channel_id=1, source_target_pairs={{0,192},{8,200},{16,208},{1,193},{9,201},{17,209},{2,194},{10,202}... | collective-permute-start | bytes 196616 | tf_op jit(solution)/shard_map/ppermute | solution.py:431
  35.1 6.4 %collective-permute-done.4 = f32[2,32,256]{2,1,0:T(8,128)S(1)} collective-permute-done((f32[2,32,256]{2,1,0:T(8,128)S(1)}, f32[2,32,256]{2,1,0:T(8,128)S(1)}, u32[]{:S(2)}, u32[]{:S(2)}) %collective-permute-start.4) | collective-permute-done | bytes 65568 | tf_op jit(solution)/shard_map/ppermute | solution.py:431
  47.1 4.5 %collective-permute-done.7.far1 = f32[9,32,256]{2,1,0:T(8,128)S(1)} collective-permute-done((f32[9,32,256]{2,1,0:T(8,128)S(1)}, f32[9,32,256]{2,1,0:T(8,128)S(1)}, u32[]{:S(2)}, u32[]{:S(2)}) %collective-permute-start.7) | collective-permute-done | bytes 294944 | tf_op jit(solution)/shard_map/ppermute | solution.py:431
  51.6 6.3 %collective-permute-done.6.far0 = f32[9,32,256]{2,1,0:T(8,128)S(1)} collective-permute-done((f32[9,32,256]{2,1,0:T(8,128)S(1)}, f32[9,32,256]{2,1,0:T(8,128)S(1)}, u32[]{:S(2)}, u32[]{:S(2)}) %collective-permute-start.6) | collective-permute-done | bytes 294944 | tf_op jit(solution)/shard_map/ppermute | solution.py:431
  58.6 11.2 %collective-permute-start.10 = (f32[2,9,32,256]{3,2,1,0:T(8,128)S(1)}, f32[2,9,32,256]{3,2,1,0:T(8,128)S(1)}, u32[]{:S(2)}, u32[]{:S(2)}) collective-permute-start(f32[2,9,32,256]{3,2,1,0:T(8,128)S(1)} %hold.1.held), channel_id=1, source_target_pairs={{0,16},{8,56},{16,32},{32,48},{40,24},{48,0},{56,40},{64,80},{72,1... | collective-permute-start | bytes 1769480 | tf_op jit(solution)/shard_map/ppermute | solution.py:431
  69.8 9.2 %collective-permute-start.9 = (f32[2,9,32,256]{3,2,1,0:T(8,128)S(1)}, f32[2,9,32,256]{3,2,1,0:T(8,128)S(1)}, u32[]{:S(2)}, u32[]{:S(2)}) collective-permute-start(f32[2,9,32,256]{3,2,1,0:T(8,128)S(1)} %hold.1.held), channel_id=1, source_target_pairs={{0,184},{8,128},{16,136},{32,152},{40,160},{48,168},{56,176},{64,2... | collective-permute-start | bytes 1769480 | tf_op jit(solution)/shard_map/ppermute | solution.py:431
  79.0 1.9 %collective-permute-start.8 = (f32[2,9,32,256]{3,2,1,0:T(8,128)S(1)}, f32[2,9,32,256]{3,2,1,0:T(8,128)}, u32[]{:S(2)}, u32[]{:S(2)}) collective-permute-start(f32[2,9,32,256]{3,2,1,0:T(8,128)S(1)} %hold.1.held), channel_id=1, source_target_pairs={{0,136},{8,144},{16,152},{32,168},{40,176},{48,184},{56,128},{64,2... | collective-permute-start | bytes 1769480 | tf_op jit(solution)/shard_map/ppermute | solution.py:431
  82.3 4.8 %collective-permute-done.10.two = f32[2,9,32,256]{3,2,1,0:T(8,128)S(1)} collective-permute-done((f32[2,9,32,256]{3,2,1,0:T(8,128)S(1)}, f32[2,9,32,256]{3,2,1,0:T(8,128)S(1)}, u32[]{:S(2)}, u32[]{:S(2)}) %collective-permute-start.10) | collective-permute-done | bytes 589856 | tf_op jit(solution)/shard_map/ppermute | solution.py:431
  87.1 16.4 %collective-permute-done.9.before = f32[2,9,32,256]{3,2,1,0:T(8,128)S(1)} collective-permute-done((f32[2,9,32,256]{3,2,1,0:T(8,128)S(1)}, f32[2,9,32,256]{3,2,1,0:T(8,128)S(1)}, u32[]{:S(2)}, u32[]{:S(2)}) %collective-permute-start.9) | collective-permute-done | bytes 589856 | tf_op jit(solution)/shard_map/ppermute | solution.py:431
  103.5 6.9 %collective-permute-done.8.after = f32[2,9,32,256]{3,2,1,0:T(8,128)} collective-permute-done((f32[2,9,32,256]{3,2,1,0:T(8,128)S(1)}, f32[2,9,32,256]{3,2,1,0:T(8,128)}, u32[]{:S(2)}, u32[]{:S(2)}) %collective-permute-start.8) | collective-permute-done | bytes 589856 | tf_op jit(solution)/shard_map/ppermute | solution.py:431
  110.4 4.0 %merge.1 = (f32[2,3,8,32,256]{4,3,2,1,0:T(8,128)}, f32[3,8,32,256]{3,2,1,0:T(8,128)}, f32[3,8,32,256]{3,2,1,0:T(8,128)}, f32[8,3,2,32,256]{4,3,2,1,0:T(8,128)}) custom-call(s32[6]{0:T(128)} %reshape_squeeze.3.found_ref, f32[2,9,32,256]{3,2,1,0:T(8,128)} %copy-done.2, f32[2,9,32,256]{3,2,1,0:T(8,128)} %collective-permute-done.8.after, ...), custom_call_target="tpu_custom_call" | custom-call | tf_op jit(solution)/shard_map/merge/pallas_call | solution.py:214
  116.0 5.4 %all-to-all-start.2 = ((f32[8,3,2,32,256]{4,3,2,1,0:T(8,128)}), f32[8,3,2,32,256]{4,3,2,1,0:T(8,128)}, u32[]{:S(2)}, u32[]{:S(2)}) async-start(f32[8,3,2,32,256]{4,3,2,1,0:T(8,128)} %get-tuple-element.28), calls=%async_computation.2 | async-start | bytes 3145728 | tf_op jit(solution)/shard_map/all_to_all | solution.py:474
  121.5 2.7 %collective-permute-start.14 = (f32[3,8,32,256]{3,2,1,0:T(8,128)}, f32[3,8,32,256]{3,2,1,0:T(8,128)}, u32[]{:S(2)}, u32[]{:S(2)}) collective-permute-start(f32[3,8,32,256]{3,2,1,0:T(8,128)} %get-tuple-element.34), channel_id=1, source_target_pairs={{0,56},{8,0},{16,8},{24,16},{32,24},{40,32},{48,40},{56,48},{64,12... | collective-permute-start | bytes 2359304 | tf_op jit(solution)/shard_map/ppermute | solution.py:431
  124.2 2.2 %copy-done = f32[2,256,8,256]{3,2,1,0:T(8,128)S(1)} copy-done((f32[2,256,8,256]{3,2,1,0:T(8,128)S(1)}, f32[2,256,8,256]{3,2,1,0:T(8,128)}, u32[]{:S(2)}) %copy-start) | copy-done | bytes 4194328
  126.3 4.2 %pack.1 = (f32[8,256,256]{2,1,0:T(8,128)S(1)}, f32[8,256,256]{2,1,0:T(8,128)S(1)}) custom-call(s32[4]{0:T(128)S(1)} %copy-done.10, s32[64,64]{1,0:T(8,128)S(1)} %copy-done.9, s32[2,256]{1,0:T(2,128)S(1)} %copy-done.11, f32[2,256,8,256]{3,2,1,0:T(8,128)S(1)} %copy-done, f32[2,3,8,32,256]{4,3,2,1,0:T(8,128)S(1)} %copy-done.1), custom_call_target="tpu_custom_call" | custom-call | tf_op jit(solution)/shard_map/pack/pallas_call | solution.py:130
  133.3 9.0 %all-to-all-done.2.corner_ref = f32[8,3,2,32,256]{4,3,2,1,0:T(8,128)} async-done(((f32[8,3,2,32,256]{4,3,2,1,0:T(8,128)}), f32[8,3,2,32,256]{4,3,2,1,0:T(8,128)}, u32[]{:S(2)}, u32[]{:S(2)}) %all-to-all-start.2) | async-done | bytes 1572896 | tf_op jit(solution)/shard_map/all_to_all | solution.py:474
  144.6 7.0 %left.1 = (bf16[512,2304]{1,0:T(8,128)(2,1)S(1)}, bf16[3,256,768]{2,1,0:T(8,128)(2,1)S(1)}, bf16[3,256,768]{2,1,0:T(8,128)(2,1)S(1)}, f32[3,2,256,256]{3,2,1,0:T(8,128)S(1)}) custom-call(s32[4]{0:T(128)S(1)} %copy-done.10, s32[64,64]{1,0:T(8,128)S(1)} %copy-done.9, f32[8,3,2,32,256]{4,3,2,1,0:T(8,128)S(1)} %all-to-all-done.1.columns_ref, ...), custom_call_target="tpu_custom_call" | custom-call | tf_op jit(solution)/shard_map/left/pallas_call | solution.py:290
  151.7 17.1 %finish.1 = f32[2,256,8,256]{3,2,1,0:T(8,128)} custom-call(s32[4]{0:T(128)S(1)} %copy-done.10, s32[64,64]{1,0:T(8,128)S(1)} %copy-done.9, f32[8,256,256]{2,1,0:T(8,128)S(1)} %copy-done.4, f32[8,256,256]{2,1,0:T(8,128)S(1)} %copy-done.6, bf16[512,2304]{1,0:T(8,128)(2,1)S(1)} %get-tuple-element.29.ll, bf16[3,256,768]{2,1,0:T(8,128)(2,1)S(1)} %get-tuple-element.30.c3, ...), custom_call_target="tpu_custom_call" | custom-call | tf_op jit(solution)/shard_map/finish/pallas_call | solution.py:407
  (59 shorter events, 19.9 us)
Async XLA Ops:
  6.7 16.1 %all-to-all-start = ((f32[8,2,32,256]{3,2,1,0:T(8,128)}), f32[8,2,32,256]{3,2,1,0:T(8,128)S(1)}, u32[]{:S(2)}, u32[]{:S(2)}) async-start(f32[8,2,32,256]{3,2,1,0:T(8,128)} %get-tuple-element.24), calls=%async_computation | async-start | bytes 1048576 | tf_op jit(solution)/shard_map/all_to_all | solution.py:454
  13.4 29.6 %collective-permute-start = (f32[2,8,32,256]{3,2,1,0:T(8,128)}, f32[2,8,32,256]{3,2,1,0:T(8,128)S(1)}, u32[]{:S(2)}, u32[]{:S(2)}) collective-permute-start(f32[2,8,32,256]{3,2,1,0:T(8,128)} %get-tuple-element.21), channel_id=1, source_target_pairs={{0,128},{8,136},{16,144},{1,129},{9,137},{17,145},{2,130},{10,138}... | collective-permute-start | bytes 1572872 | tf_op jit(solution)/shard_map/ppermute | solution.py:431
  17.4 25.6 %collective-permute-start.1 = (f32[2,8,32,256]{3,2,1,0:T(8,128)}, f32[2,8,32,256]{3,2,1,0:T(8,128)}, u32[]{:S(2)}, u32[]{:S(2)}) collective-permute-start(f32[2,8,32,256]{3,2,1,0:T(8,128)} %get-tuple-element.22), channel_id=1, source_target_pairs={{0,64},{8,72},{16,80},{1,65},{9,73},{17,81},{2,66},{10,74},{18,82}... | collective-permute-start | bytes 1572872 | tf_op jit(solution)/shard_map/ppermute | solution.py:431
  19.5 23.5 %collective-permute-start.2 = (f32[2,8,32,256]{3,2,1,0:T(8,128)}, f32[2,8,32,256]{3,2,1,0:T(8,128)}, u32[]{:S(2)}, u32[]{:S(2)}) collective-permute-start(f32[2,8,32,256]{3,2,1,0:T(8,128)} %get-tuple-element.23), channel_id=1, source_target_pairs={{0,192},{8,200},{16,208},{1,193},{9,201},{17,209},{2,194},{10,202}... | collective-permute-start | bytes 1572872 | tf_op jit(solution)/shard_map/ppermute | solution.py:431
  24.2 18.8 %copy-start.14 = (f32[2,8,32,256]{3,2,1,0:T(8,128)S(1)}, f32[2,8,32,256]{3,2,1,0:T(8,128)}, u32[]{:S(2)}) copy-start(f32[2,8,32,256]{3,2,1,0:T(8,128)} %get-tuple-element.20) | copy-start | bytes 1572868
  24.2 33.7 %all-to-all-start.1 = ((f32[8,3,2,32,256]{4,3,2,1,0:T(8,128)}), f32[8,3,2,32,256]{4,3,2,1,0:T(8,128)S(1)}, u32[]{:S(2)}, u32[]{:S(2)}) async-start(f32[8,3,2,32,256]{4,3,2,1,0:T(8,128)} %broadcast_in_dim.7), calls=%async_computation.1 | async-start | bytes 3145728 | tf_op jit(solution)/shard_map/all_to_all | solution.py:436
  28.8 5.1 %collective-permute-start.5 = (f32[2,32,256]{2,1,0:T(8,128)S(1)}, f32[2,32,256]{2,1,0:T(8,128)S(1)}, u32[]{:S(2)}, u32[]{:S(2)}) collective-permute-start(f32[2,32,256]{2,1,0:T(8,128)S(1)} %pad_maximum_fusion.1), channel_id=1, source_target_pairs={{0,192},{8,200},{16,208},{1,193},{9,201},{17,209},{2,194},{10,202}... | collective-permute-start | bytes 196616 | tf_op jit(solution)/shard_map/ppermute | solution.py:431
  32.5 9.1 %collective-permute-start.4 = (f32[2,32,256]{2,1,0:T(8,128)S(1)}, f32[2,32,256]{2,1,0:T(8,128)S(1)}, u32[]{:S(2)}, u32[]{:S(2)}) collective-permute-start(f32[2,32,256]{2,1,0:T(8,128)S(1)} %pad_maximum_fusion.1), channel_id=1, source_target_pairs={{0,64},{8,72},{16,80},{1,65},{9,73},{17,81},{2,66},{10,74},{18,82}... | collective-permute-start | bytes 196616 | tf_op jit(solution)/shard_map/ppermute | solution.py:431
  33.8 9.2 %collective-permute-start.3 = (f32[2,32,256]{2,1,0:T(8,128)S(1)}, f32[2,32,256]{2,1,0:T(8,128)S(1)}, u32[]{:S(2)}, u32[]{:S(2)}) collective-permute-start(f32[2,32,256]{2,1,0:T(8,128)S(1)} %pad_maximum_fusion.1), channel_id=1, source_target_pairs={{0,128},{8,136},{16,144},{1,129},{9,137},{17,145},{2,130},{10,138}... | collective-permute-start | bytes 196616 | tf_op jit(solution)/shard_map/ppermute | solution.py:431
  44.4 13.5 %copy-start.10 = (s32[4]{0:T(128)S(1)}, s32[4]{0:T(128)}, u32[]{:S(2)}) copy-start(s32[4]{0:T(128)} %pad_add_fusion.where_ref) | copy-start | bytes 52
  44.4 7.1 %collective-permute-start.7 = (f32[9,32,256]{2,1,0:T(8,128)S(1)}, f32[9,32,256]{2,1,0:T(8,128)S(1)}, u32[]{:S(2)}, u32[]{:S(2)}) collective-permute-start(f32[9,32,256]{2,1,0:T(8,128)S(1)} %get-tuple-element.35), channel_id=1, source_target_pairs={{0,32},{8,40},{16,184},{64,96},{72,104},{80,248},{128,160},{136,16... | collective-permute-start | bytes 884744 | tf_op jit(solution)/shard_map/ppermute | solution.py:431
  45.8 12.2 %collective-permute-start.6 = (f32[9,32,256]{2,1,0:T(8,128)S(1)}, f32[9,32,256]{2,1,0:T(8,128)S(1)}, u32[]{:S(2)}, u32[]{:S(2)}) collective-permute-start(f32[9,32,256]{2,1,0:T(8,128)S(1)} %get-tuple-element.36), channel_id=1, source_target_pairs={{0,32},{8,40},{16,48},{64,96},{72,104},{80,112},{128,160},{136,168... | collective-permute-start | bytes 884744 | tf_op jit(solution)/shard_map/ppermute | solution.py:431
  58.6 51.8 %copy-start.2 = (f32[2,9,32,256]{3,2,1,0:T(8,128)}, f32[2,9,32,256]{3,2,1,0:T(8,128)S(1)}, u32[]{:S(2)}) copy-start(f32[2,9,32,256]{3,2,1,0:T(8,128)S(1)} %hold.1.held) | copy-start | bytes 1769476
  58.6 28.5 %collective-permute-start.10 = (f32[2,9,32,256]{3,2,1,0:T(8,128)S(1)}, f32[2,9,32,256]{3,2,1,0:T(8,128)S(1)}, u32[]{:S(2)}, u32[]{:S(2)}) collective-permute-start(f32[2,9,32,256]{3,2,1,0:T(8,128)S(1)} %hold.1.held), channel_id=1, source_target_pairs={{0,16},{8,56},{16,32},{32,48},{40,24},{48,0},{56,40},{64,80},{72,1... | collective-permute-start | bytes 1769480 | tf_op jit(solution)/shard_map/ppermute | solution.py:431
  69.8 33.7 %collective-permute-start.9 = (f32[2,9,32,256]{3,2,1,0:T(8,128)S(1)}, f32[2,9,32,256]{3,2,1,0:T(8,128)S(1)}, u32[]{:S(2)}, u32[]{:S(2)}) collective-permute-start(f32[2,9,32,256]{3,2,1,0:T(8,128)S(1)} %hold.1.held), channel_id=1, source_target_pairs={{0,184},{8,128},{16,136},{32,152},{40,160},{48,168},{56,176},{64,2... | collective-permute-start | bytes 1769480 | tf_op jit(solution)/shard_map/ppermute | solution.py:431
  79.0 31.4 %collective-permute-start.8 = (f32[2,9,32,256]{3,2,1,0:T(8,128)S(1)}, f32[2,9,32,256]{3,2,1,0:T(8,128)}, u32[]{:S(2)}, u32[]{:S(2)}) collective-permute-start(f32[2,9,32,256]{3,2,1,0:T(8,128)S(1)} %hold.1.held), channel_id=1, source_target_pairs={{0,136},{8,144},{16,152},{32,168},{40,176},{48,184},{56,128},{64,2... | collective-permute-start | bytes 1769480 | tf_op jit(solution)/shard_map/ppermute | solution.py:431
  87.1 23.3 %copy-start.12 = (f32[2,9,32,256]{3,2,1,0:T(8,128)}, f32[2,9,32,256]{3,2,1,0:T(8,128)S(1)}, u32[]{:S(2)}) copy-start(f32[2,9,32,256]{3,2,1,0:T(8,128)S(1)} %collective-permute-done.10.two) | copy-start | bytes 1769476
  114.5 37.1 %collective-permute-start.12 = (f32[2,3,8,32,256]{4,3,2,1,0:T(8,128)}, f32[2,3,8,32,256]{4,3,2,1,0:T(8,128)}, u32[]{:S(2)}, u32[]{:S(2)}) collective-permute-start(f32[2,3,8,32,256]{4,3,2,1,0:T(8,128)} %get-tuple-element.25.after_ref.mine), channel_id=1, source_target_pairs={{0,192},{8,200},{16,208},{24,216},{32,224},{40,232},{48,240},{56,2... | collective-permute-start | bytes 4718600 | tf_op jit(solution)/shard_map/ppermute | solution.py:431
  114.6 37.0 %collective-permute-start.11 = (f32[2,3,8,32,256]{4,3,2,1,0:T(8,128)}, f32[2,3,8,32,256]{4,3,2,1,0:T(8,128)}, u32[]{:S(2)}, u32[]{:S(2)}) collective-permute-start(f32[2,3,8,32,256]{4,3,2,1,0:T(8,128)} %get-tuple-element.25.after_ref.mine), channel_id=1, source_target_pairs={{0,64},{8,72},{16,80},{24,88},{32,96},{40,104},{48,112},{56,120},{... | collective-permute-start | bytes 4718600 | tf_op jit(solution)/shard_map/ppermute | solution.py:431
  116.0 8.1 %copy-start.9 = (s32[64,64]{1,0:T(8,128)S(1)}, s32[64,64]{1,0:T(8,128)}, u32[]{:S(2)}) copy-start(s32[64,64]{1,0:T(8,128)} %pattern_ref.7) | copy-start | bytes 49156
  116.0 8.1 %copy-start.11 = (s32[2,256]{1,0:T(2,128)S(1)}, s32[2,256]{1,0:T(2,128)}, u32[]{:S(2)}) copy-start(s32[2,256]{1,0:T(2,128)} %perm_ref.3) | copy-start | bytes 6148
  116.0 26.3 %all-to-all-start.2 = ((f32[8,3,2,32,256]{4,3,2,1,0:T(8,128)}), f32[8,3,2,32,256]{4,3,2,1,0:T(8,128)}, u32[]{:S(2)}, u32[]{:S(2)}) async-start(f32[8,3,2,32,256]{4,3,2,1,0:T(8,128)} %get-tuple-element.28), calls=%async_computation.2 | async-start | bytes 3145728 | tf_op jit(solution)/shard_map/all_to_all | solution.py:474
  121.5 30.1 %collective-permute-start.13 = (f32[3,8,32,256]{3,2,1,0:T(8,128)}, f32[3,8,32,256]{3,2,1,0:T(8,128)}, u32[]{:S(2)}, u32[]{:S(2)}) collective-permute-start(f32[3,8,32,256]{3,2,1,0:T(8,128)} %get-tuple-element.33), channel_id=1, source_target_pairs={{0,8},{8,16},{16,24},{24,32},{32,40},{40,48},{48,56},{56,0},{64,72... | collective-permute-start | bytes 2359304 | tf_op jit(solution)/shard_map/ppermute | solution.py:431
  121.5 30.1 %collective-permute-start.14 = (f32[3,8,32,256]{3,2,1,0:T(8,128)}, f32[3,8,32,256]{3,2,1,0:T(8,128)}, u32[]{:S(2)}, u32[]{:S(2)}) collective-permute-start(f32[3,8,32,256]{3,2,1,0:T(8,128)} %get-tuple-element.34), channel_id=1, source_target_pairs={{0,56},{8,0},{16,8},{24,16},{32,24},{40,32},{48,40},{56,48},{64,12... | collective-permute-start | bytes 2359304 | tf_op jit(solution)/shard_map/ppermute | solution.py:431
  (9 other events, 36.3 us)

commit v4 on v3

--- a/solution.py
+++ b/solution.py
@@ -170,7 +170,7 @@
 
 def merge_body(
     found_ref, held, after, before, two,
-    all_ref, half0, half1, corner_ref, stage, slices, sem,
+    all_ref, corner_ref, stage, slices, sem,
 ):
     pieces = [(r, h) for r in range(3) for h in range(2)]
     arrive = []
@@ -191,37 +191,31 @@
     small, last = [], []
     for n, (r, h) in enumerate(pieces):
         arrive[n].wait()
-        k = 6 + 3 * n
-        last.append(pltpu.make_async_copy(stage.at[h, r, eight], all_ref.at[h, r], sem.at[k]))
         last.append(
-            pltpu.make_async_copy(stage.at[h, r, eight], (half0, half1)[h].at[r], sem.at[k + 1])
+            pltpu.make_async_copy(stage.at[h, r, eight], all_ref.at[h, r], sem.at[6 + 2 * n])
         )
-        small.append(pltpu.make_async_copy(stage.at[h, r, 8], slices.at[r, h], sem.at[k + 2]))
-        last[-2].start()
+        small.append(pltpu.make_async_copy(stage.at[h, r, 8], slices.at[r, h], sem.at[7 + 2 * n]))
         last[-1].start()
         small[-1].start()
     for one in small:
         one.wait()
     for q in range(8):
-        last.append(pltpu.make_async_copy(slices, corner_ref.at[q], sem.at[24 + q]))
+        last.append(pltpu.make_async_copy(slices, corner_ref.at[q], sem.at[18 + q]))
         last[-1].start()
     for one in last:
         one.wait()
 
 
 def merge(found, *parts):
-    half = shaped((3, 8, 32, 256), F32)
     return pl.pallas_call(
         merge_body,
         in_specs=[SMEM] + [ANY] * 4,
-        out_specs=[ANY] * 4,
-        out_shape=[
-            shaped((2, 3, 8, 32, 256), F32), half, half, shaped((8, 3, 2, 32, 256), F32)
-        ],
+        out_specs=[ANY] * 2,
+        out_shape=[shaped((2, 3, 8, 32, 256), F32), shaped((8, 3, 2, 32, 256), F32)],
         scratch_shapes=[
             VMEM((2, 3, 9, 32, 256), F32),
             VMEM((3, 2, 32, 256), F32),
-            pltpu.SemaphoreType.DMA((32,)),
+            pltpu.SemaphoreType.DMA((26,)),
         ],
         compiler_params=params(58),
         name="merge",
@@ -308,7 +302,7 @@
 
 
 def finish_body(
-    where_ref, pattern_ref, ap0, ap1, ll, c3, li, raw, mine, lower, higher, half0, half1,
+    where_ref, pattern_ref, ap0, ap1, ll, c3, li, raw, mine, lower, higher, below,
     out_ref, panel, upper, out, sem,
 ):
     prow, pcol, turn = where_ref[0], where_ref[1], where_ref[2]
@@ -321,7 +315,7 @@
         return one
 
     starts = [pl.multiple_of(lax.rem(turn + s, 4) * 64, 64) for s in SHIFTS]
-    halves = [ref.at[h] for ref in (mine, lower, higher) for h in range(2)] + [half0, half1]
+    halves = [ref.at[h] for ref in (mine, lower, higher, below) for h in range(2)]
 
     def panels(n):
         lo, hi = RANGES[n]
@@ -406,7 +400,7 @@
 def finish(where, pattern, ap0, ap1, ll, c3, li, raw, *mains):
     return pl.pallas_call(
         finish_body,
-        in_specs=[SMEM, SMEM] + [HERE] * 6 + [ANY] * 5,
+        in_specs=[SMEM, SMEM] + [HERE] * 6 + [ANY] * 4,
         out_specs=ANY,
         out_shape=shaped((2, 256, 8, 256), F32),
         scratch_shapes=[
@@ -470,13 +464,13 @@
     steps = [(0, 2), (0, -2), (0, 2), None, (0, 2), (0, -2), (0, 2), (0, -2)]
     two = hop(both, steps, lambda x, z: z != 3)
     found = jnp.array(PICK, jnp.int32)[:, :, z].reshape(6)
-    mine, half0, half1, corner = merge(found, both, after, before, two)
+    mine, corner = merge(found, both, after, before, two)
     corner = lax.all_to_all(corner, "pcol", 0, 0)
     ap0, ap1 = pack(where, pattern, row_perm, matrix, mine)
     lower, higher = hop(mine, [(1, 0)]), hop(mine, [(-1, 0)])
-    half0, half1 = hop(half0, [(0, 1)]), hop(half1, [(0, -1)])
+    below = hop(mine, [(0, 1)])
     ll, c3, li, raw = left(where, pattern, columns, corner, lower_inv, upper_inv)
-    return finish(where, pattern, ap0, ap1, ll, c3, li, raw, mine, lower, higher, half0, half1)
+    return finish(where, pattern, ap0, ap1, ll, c3, li, raw, mine, lower, higher, below)
 
 
 def solution(mesh):

time: 170 us -> 170 us (level)
  waiting for transfers between devices: 57.1 us -> 59.8 us
  starting transfers between devices: 60.2 us -> 57.6 us
    all_to_all x1, waiting for transfers between devices: 9.03 us -> 11.7 us  [on_device(): corner = lax.all_to_all(corner, 'pcol', 0, 0)]
    ppermute x15 -> x14, starting transfers between devices: 43.7 us -> 41.1 us  [hop(): return lax.ppermute(array, 'prow', pairs)]
    ppermute x15 -> x14, waiting for transfers between devices: 46.8 us -> 46.8 us  [hop(): return lax.ppermute(array, 'prow', pairs)]
  transfers between devices with their start and end apart: 18 -> 17, of which waited for: 9 -> 9; matrix products, arithmetic and copies ran while one was open for 2% -> 2% of each run, Pallas kernels for 7% -> 7%
where the time goes in v4:
time: 170 us; the launch traced here: 169 us
  waiting for transfers between devices  59.8 us (35%)
  starting transfers between devices  57.6 us (34%)
  Pallas kernels  38.8 us (23%)
  local copies, waits for them, and re-layouts  9.78 us (6%)
  other arithmetic  2.15 us (1%)
    ppermute x14, waiting for transfers between devices, hop(): return lax.ppermute(array, 'prow', pairs)  46.8 us
    ppermute x14, starting transfers between devices, hop(): return lax.ppermute(array, 'prow', pairs)  41.1 us
    pallas_call x1, Pallas kernels, finish(): pl.pallas_call(finish_body, in_specs=[SMEM, SMEM] + [HERE] * 6 + [ANY] *...  17.1 us
    all_to_all x1, waiting for transfers between devices, on_device(): corner = lax.all_to_all(corner, 'pcol', 0, 0)  11.7 us
    unnamed x30, local copies, waits for them, and re-layouts  7.16 us
    pallas_call x1, Pallas kernels, left(): pl.pallas_call(left_body, in_specs=[SMEM, SMEM, ANY, ANY, ANY, ANY], out_...  7.01 us
    all_to_all x1, starting transfers between devices, on_device(): faces = lax.all_to_all(faces, 'pcol', 0, 0)  6.65 us
    pallas_call x1, Pallas kernels, pack_first(): pl.pallas_call(pack_first_body, in_specs=[SMEM, SMEM, SMEM, ANY], out_spe...  6.14 us
  transfers between devices with their start and end apart: 17, of which 9 were waited for; matrix products, arithmetic and copies ran while one was open for 2% of the time, Pallas kernels for 7%

profile of v4, /device:TPU:1, one launch (start us, length us, event | category | flops | bytes accessed | tf_op | source)
XLA Modules:
  0.0 168.6 jit_solution(12455927700826362681)
XLA Ops:
  0.7 6.1 %pack_first.1 = (f32[8,2,32,256]{3,2,1,0:T(8,128)}, f32[2,8,32,256]{3,2,1,0:T(8,128)}, f32[2,8,32,256]{3,2,1,0:T(8,128)}, f32[2,8,32,256]{3,2,1,0:T(8,128)}, f32[2,8,32,256]{3,2,1,0:T(8,128)}) custom-call(s32[4]{0:T(128)} %pad_add_fusion.where_ref, s32[64,64]{1,0:T(8,128)} %pattern_ref.7, s32[2,256]{1,0:T(2,128)} %perm_ref.3, f32[2,256,8,256]{3,2,1,0:T(8,128)} %a_ref.3), custom_call_target="tpu_custom_call" | custom-call | tf_op jit(solution)/shard_map/pack_first/pallas_call | solution.py:106
  6.8 6.6 %all-to-all-start = ((f32[8,2,32,256]{3,2,1,0:T(8,128)}), f32[8,2,32,256]{3,2,1,0:T(8,128)S(1)}, u32[]{:S(2)}, u32[]{:S(2)}) async-start(f32[8,2,32,256]{3,2,1,0:T(8,128)} %get-tuple-element.22), calls=%async_computation | async-start | bytes 1048576 | tf_op jit(solution)/shard_map/all_to_all | solution.py:448
  13.5 4.0 %collective-permute-start = (f32[2,8,32,256]{3,2,1,0:T(8,128)}, f32[2,8,32,256]{3,2,1,0:T(8,128)S(1)}, u32[]{:S(2)}, u32[]{:S(2)}) collective-permute-start(f32[2,8,32,256]{3,2,1,0:T(8,128)} %get-tuple-element.19), channel_id=1, source_target_pairs={{0,128},{8,136},{16,144},{1,129},{9,137},{17,145},{2,130},{10,138}... | collective-permute-start | bytes 1572872 | tf_op jit(solution)/shard_map/ppermute | solution.py:425
  17.5 2.1 %collective-permute-start.1 = (f32[2,8,32,256]{3,2,1,0:T(8,128)}, f32[2,8,32,256]{3,2,1,0:T(8,128)}, u32[]{:S(2)}, u32[]{:S(2)}) collective-permute-start(f32[2,8,32,256]{3,2,1,0:T(8,128)} %get-tuple-element.20), channel_id=1, source_target_pairs={{0,64},{8,72},{16,80},{1,65},{9,73},{17,81},{2,66},{10,74},{18,82}... | collective-permute-start | bytes 1572872 | tf_op jit(solution)/shard_map/ppermute | solution.py:425
  19.6 2.1 %collective-permute-start.2 = (f32[2,8,32,256]{3,2,1,0:T(8,128)}, f32[2,8,32,256]{3,2,1,0:T(8,128)}, u32[]{:S(2)}, u32[]{:S(2)}) collective-permute-start(f32[2,8,32,256]{3,2,1,0:T(8,128)} %get-tuple-element.21), channel_id=1, source_target_pairs={{0,192},{8,200},{16,208},{1,193},{9,201},{17,209},{2,194},{10,202}... | collective-permute-start | bytes 1572872 | tf_op jit(solution)/shard_map/ppermute | solution.py:425
  24.3 4.5 %all-to-all-start.1 = ((f32[8,3,2,32,256]{4,3,2,1,0:T(8,128)}), f32[8,3,2,32,256]{4,3,2,1,0:T(8,128)S(1)}, u32[]{:S(2)}, u32[]{:S(2)}) async-start(f32[8,3,2,32,256]{4,3,2,1,0:T(8,128)} %broadcast_in_dim.7), calls=%async_computation.1 | async-start | bytes 3145728 | tf_op jit(solution)/shard_map/all_to_all | solution.py:430
  28.8 3.7 %collective-permute-start.5 = (f32[2,32,256]{2,1,0:T(8,128)S(1)}, f32[2,32,256]{2,1,0:T(8,128)S(1)}, u32[]{:S(2)}, u32[]{:S(2)}) collective-permute-start(f32[2,32,256]{2,1,0:T(8,128)S(1)} %pad_maximum_fusion.1), channel_id=1, source_target_pairs={{0,192},{8,200},{16,208},{1,193},{9,201},{17,209},{2,194},{10,202}... | collective-permute-start | bytes 196616 | tf_op jit(solution)/shard_map/ppermute | solution.py:425
  35.2 6.4 %collective-permute-done.4 = f32[2,32,256]{2,1,0:T(8,128)S(1)} collective-permute-done((f32[2,32,256]{2,1,0:T(8,128)S(1)}, f32[2,32,256]{2,1,0:T(8,128)S(1)}, u32[]{:S(2)}, u32[]{:S(2)}) %collective-permute-start.4) | collective-permute-done | bytes 65568 | tf_op jit(solution)/shard_map/ppermute | solution.py:425
  47.2 4.5 %collective-permute-done.7.far1 = f32[9,32,256]{2,1,0:T(8,128)S(1)} collective-permute-done((f32[9,32,256]{2,1,0:T(8,128)S(1)}, f32[9,32,256]{2,1,0:T(8,128)S(1)}, u32[]{:S(2)}, u32[]{:S(2)}) %collective-permute-start.7) | collective-permute-done | bytes 294944 | tf_op jit(solution)/shard_map/ppermute | solution.py:425
  51.7 6.3 %collective-permute-done.6.far0 = f32[9,32,256]{2,1,0:T(8,128)S(1)} collective-permute-done((f32[9,32,256]{2,1,0:T(8,128)S(1)}, f32[9,32,256]{2,1,0:T(8,128)S(1)}, u32[]{:S(2)}, u32[]{:S(2)}) %collective-permute-start.6) | collective-permute-done | bytes 294944 | tf_op jit(solution)/shard_map/ppermute | solution.py:425
  58.7 11.2 %collective-permute-start.10 = (f32[2,9,32,256]{3,2,1,0:T(8,128)S(1)}, f32[2,9,32,256]{3,2,1,0:T(8,128)S(1)}, u32[]{:S(2)}, u32[]{:S(2)}) collective-permute-start(f32[2,9,32,256]{3,2,1,0:T(8,128)S(1)} %hold.1.held), channel_id=1, source_target_pairs={{0,16},{8,56},{16,32},{32,48},{40,24},{48,0},{56,40},{64,80},{72,1... | collective-permute-start | bytes 1769480 | tf_op jit(solution)/shard_map/ppermute | solution.py:425
  69.9 9.2 %collective-permute-start.9 = (f32[2,9,32,256]{3,2,1,0:T(8,128)S(1)}, f32[2,9,32,256]{3,2,1,0:T(8,128)S(1)}, u32[]{:S(2)}, u32[]{:S(2)}) collective-permute-start(f32[2,9,32,256]{3,2,1,0:T(8,128)S(1)} %hold.1.held), channel_id=1, source_target_pairs={{0,184},{8,128},{16,136},{32,152},{40,160},{48,168},{56,176},{64,2... | collective-permute-start | bytes 1769480 | tf_op jit(solution)/shard_map/ppermute | solution.py:425
  79.1 1.9 %collective-permute-start.8 = (f32[2,9,32,256]{3,2,1,0:T(8,128)S(1)}, f32[2,9,32,256]{3,2,1,0:T(8,128)}, u32[]{:S(2)}, u32[]{:S(2)}) collective-permute-start(f32[2,9,32,256]{3,2,1,0:T(8,128)S(1)} %hold.1.held), channel_id=1, source_target_pairs={{0,136},{8,144},{16,152},{32,168},{40,176},{48,184},{56,128},{64,2... | collective-permute-start | bytes 1769480 | tf_op jit(solution)/shard_map/ppermute | solution.py:425
  82.3 4.9 %collective-permute-done.10.two = f32[2,9,32,256]{3,2,1,0:T(8,128)S(1)} collective-permute-done((f32[2,9,32,256]{3,2,1,0:T(8,128)S(1)}, f32[2,9,32,256]{3,2,1,0:T(8,128)S(1)}, u32[]{:S(2)}, u32[]{:S(2)}) %collective-permute-start.10) | collective-permute-done | bytes 589856 | tf_op jit(solution)/shard_map/ppermute | solution.py:425
  87.2 16.4 %collective-permute-done.9.before = f32[2,9,32,256]{3,2,1,0:T(8,128)S(1)} collective-permute-done((f32[2,9,32,256]{3,2,1,0:T(8,128)S(1)}, f32[2,9,32,256]{3,2,1,0:T(8,128)S(1)}, u32[]{:S(2)}, u32[]{:S(2)}) %collective-permute-start.9) | collective-permute-done | bytes 589856 | tf_op jit(solution)/shard_map/ppermute | solution.py:425
  103.6 6.9 %collective-permute-done.8.after = f32[2,9,32,256]{3,2,1,0:T(8,128)} collective-permute-done((f32[2,9,32,256]{3,2,1,0:T(8,128)S(1)}, f32[2,9,32,256]{3,2,1,0:T(8,128)}, u32[]{:S(2)}, u32[]{:S(2)}) %collective-permute-start.8) | collective-permute-done | bytes 589856 | tf_op jit(solution)/shard_map/ppermute | solution.py:425
  110.5 3.6 %merge.1 = (f32[2,3,8,32,256]{4,3,2,1,0:T(8,128)}, f32[8,3,2,32,256]{4,3,2,1,0:T(8,128)}) custom-call(s32[6]{0:T(128)} %reshape_squeeze.3.found_ref, f32[2,9,32,256]{3,2,1,0:T(8,128)} %copy-done.2, f32[2,9,32,256]{3,2,1,0:T(8,128)} %collective-permute-done.8.after, f32[2,9,32,256]{3,2,1,0:T(8,128)} %copy-done.13, f32[2,9,32,256]{3,2,1,0:T(8,128)} %copy-done.12), custom_call_target="tpu_custom_call" | custom-call | tf_op jit(solution)/shard_map/merge/pallas_call | solution.py:210
  114.3 1.5 collective-permute-start.11
  115.7 5.4 %all-to-all-start.2 = ((f32[8,3,2,32,256]{4,3,2,1,0:T(8,128)}), f32[8,3,2,32,256]{4,3,2,1,0:T(8,128)}, u32[]{:S(2)}, u32[]{:S(2)}) async-start(f32[8,3,2,32,256]{4,3,2,1,0:T(8,128)} %get-tuple-element.26), calls=%async_computation.2 | async-start | bytes 3145728 | tf_op jit(solution)/shard_map/all_to_all | solution.py:468
  121.2 2.2 %copy-done = f32[2,256,8,256]{3,2,1,0:T(8,128)S(1)} copy-done((f32[2,256,8,256]{3,2,1,0:T(8,128)S(1)}, f32[2,256,8,256]{3,2,1,0:T(8,128)}, u32[]{:S(2)}) %copy-start) | copy-done | bytes 4194328
  123.4 4.2 %pack.1 = (f32[8,256,256]{2,1,0:T(8,128)S(1)}, f32[8,256,256]{2,1,0:T(8,128)S(1)}) custom-call(s32[4]{0:T(128)S(1)} %copy-done.10, s32[64,64]{1,0:T(8,128)S(1)} %copy-done.9, s32[2,256]{1,0:T(2,128)S(1)} %copy-done.11, f32[2,256,8,256]{3,2,1,0:T(8,128)S(1)} %copy-done, f32[2,3,8,32,256]{4,3,2,1,0:T(8,128)S(1)} %copy-done.1), custom_call_target="tpu_custom_call" | custom-call | tf_op jit(solution)/shard_map/pack/pallas_call | solution.py:130
  130.3 11.7 %all-to-all-done.2.corner_ref = f32[8,3,2,32,256]{4,3,2,1,0:T(8,128)} async-done(((f32[8,3,2,32,256]{4,3,2,1,0:T(8,128)}), f32[8,3,2,32,256]{4,3,2,1,0:T(8,128)}, u32[]{:S(2)}, u32[]{:S(2)}) %all-to-all-start.2) | async-done | bytes 1572896 | tf_op jit(solution)/shard_map/all_to_all | solution.py:468
  144.3 7.0 %left.1 = (bf16[512,2304]{1,0:T(8,128)(2,1)S(1)}, bf16[3,256,768]{2,1,0:T(8,128)(2,1)S(1)}, bf16[3,256,768]{2,1,0:T(8,128)(2,1)S(1)}, f32[3,2,256,256]{3,2,1,0:T(8,128)S(1)}) custom-call(s32[4]{0:T(128)S(1)} %copy-done.10, s32[64,64]{1,0:T(8,128)S(1)} %copy-done.9, f32[8,3,2,32,256]{4,3,2,1,0:T(8,128)S(1)} %all-to-all-done.1.columns_ref, ...), custom_call_target="tpu_custom_call" | custom-call | tf_op jit(solution)/shard_map/left/pallas_call | solution.py:284
  151.3 17.1 %finish.1 = f32[2,256,8,256]{3,2,1,0:T(8,128)} custom-call(s32[4]{0:T(128)S(1)} %copy-done.10, s32[64,64]{1,0:T(8,128)S(1)} %copy-done.9, f32[8,256,256]{2,1,0:T(8,128)S(1)} %copy-done.4, f32[8,256,256]{2,1,0:T(8,128)S(1)} %copy-done.6, bf16[512,2304]{1,0:T(8,128)(2,1)S(1)} %get-tuple-element.27.ll, bf16[3,256,768]{2,1,0:T(8,128)(2,1)S(1)} %get-tuple-element.28.c3, ...), custom_call_target="tpu_custom_call" | custom-call | tf_op jit(solution)/shard_map/finish/pallas_call | solution.py:401
  (57 shorter events, 18.5 us)
Async XLA Ops:
  6.8 16.1 %all-to-all-start = ((f32[8,2,32,256]{3,2,1,0:T(8,128)}), f32[8,2,32,256]{3,2,1,0:T(8,128)S(1)}, u32[]{:S(2)}, u32[]{:S(2)}) async-start(f32[8,2,32,256]{3,2,1,0:T(8,128)} %get-tuple-element.22), calls=%async_computation | async-start | bytes 1048576 | tf_op jit(solution)/shard_map/all_to_all | solution.py:448
  13.5 29.6 %collective-permute-start = (f32[2,8,32,256]{3,2,1,0:T(8,128)}, f32[2,8,32,256]{3,2,1,0:T(8,128)S(1)}, u32[]{:S(2)}, u32[]{:S(2)}) collective-permute-start(f32[2,8,32,256]{3,2,1,0:T(8,128)} %get-tuple-element.19), channel_id=1, source_target_pairs={{0,128},{8,136},{16,144},{1,129},{9,137},{17,145},{2,130},{10,138}... | collective-permute-start | bytes 1572872 | tf_op jit(solution)/shard_map/ppermute | solution.py:425
  17.5 25.6 %collective-permute-start.1 = (f32[2,8,32,256]{3,2,1,0:T(8,128)}, f32[2,8,32,256]{3,2,1,0:T(8,128)}, u32[]{:S(2)}, u32[]{:S(2)}) collective-permute-start(f32[2,8,32,256]{3,2,1,0:T(8,128)} %get-tuple-element.20), channel_id=1, source_target_pairs={{0,64},{8,72},{16,80},{1,65},{9,73},{17,81},{2,66},{10,74},{18,82}... | collective-permute-start | bytes 1572872 | tf_op jit(solution)/shard_map/ppermute | solution.py:425
  19.6 23.5 %collective-permute-start.2 = (f32[2,8,32,256]{3,2,1,0:T(8,128)}, f32[2,8,32,256]{3,2,1,0:T(8,128)}, u32[]{:S(2)}, u32[]{:S(2)}) collective-permute-start(f32[2,8,32,256]{3,2,1,0:T(8,128)} %get-tuple-element.21), channel_id=1, source_target_pairs={{0,192},{8,200},{16,208},{1,193},{9,201},{17,209},{2,194},{10,202}... | collective-permute-start | bytes 1572872 | tf_op jit(solution)/shard_map/ppermute | solution.py:425
  24.3 18.8 %copy-start.14 = (f32[2,8,32,256]{3,2,1,0:T(8,128)S(1)}, f32[2,8,32,256]{3,2,1,0:T(8,128)}, u32[]{:S(2)}) copy-start(f32[2,8,32,256]{3,2,1,0:T(8,128)} %get-tuple-element.18) | copy-start | bytes 1572868
  24.3 33.7 %all-to-all-start.1 = ((f32[8,3,2,32,256]{4,3,2,1,0:T(8,128)}), f32[8,3,2,32,256]{4,3,2,1,0:T(8,128)S(1)}, u32[]{:S(2)}, u32[]{:S(2)}) async-start(f32[8,3,2,32,256]{4,3,2,1,0:T(8,128)} %broadcast_in_dim.7), calls=%async_computation.1 | async-start | bytes 3145728 | tf_op jit(solution)/shard_map/all_to_all | solution.py:430
  28.8 5.1 %collective-permute-start.5 = (f32[2,32,256]{2,1,0:T(8,128)S(1)}, f32[2,32,256]{2,1,0:T(8,128)S(1)}, u32[]{:S(2)}, u32[]{:S(2)}) collective-permute-start(f32[2,32,256]{2,1,0:T(8,128)S(1)} %pad_maximum_fusion.1), channel_id=1, source_target_pairs={{0,192},{8,200},{16,208},{1,193},{9,201},{17,209},{2,194},{10,202}... | collective-permute-start | bytes 196616 | tf_op jit(solution)/shard_map/ppermute | solution.py:425
  32.6 9.1 %collective-permute-start.4 = (f32[2,32,256]{2,1,0:T(8,128)S(1)}, f32[2,32,256]{2,1,0:T(8,128)S(1)}, u32[]{:S(2)}, u32[]{:S(2)}) collective-permute-start(f32[2,32,256]{2,1,0:T(8,128)S(1)} %pad_maximum_fusion.1), channel_id=1, source_target_pairs={{0,64},{8,72},{16,80},{1,65},{9,73},{17,81},{2,66},{10,74},{18,82}... | collective-permute-start | bytes 196616 | tf_op jit(solution)/shard_map/ppermute | solution.py:425
  33.9 9.2 %collective-permute-start.3 = (f32[2,32,256]{2,1,0:T(8,128)S(1)}, f32[2,32,256]{2,1,0:T(8,128)S(1)}, u32[]{:S(2)}, u32[]{:S(2)}) collective-permute-start(f32[2,32,256]{2,1,0:T(8,128)S(1)} %pad_maximum_fusion.1), channel_id=1, source_target_pairs={{0,128},{8,136},{16,144},{1,129},{9,137},{17,145},{2,130},{10,138}... | collective-permute-start | bytes 196616 | tf_op jit(solution)/shard_map/ppermute | solution.py:425
  44.5 13.5 %copy-start.10 = (s32[4]{0:T(128)S(1)}, s32[4]{0:T(128)}, u32[]{:S(2)}) copy-start(s32[4]{0:T(128)} %pad_add_fusion.where_ref) | copy-start | bytes 52
  44.5 7.1 %collective-permute-start.7 = (f32[9,32,256]{2,1,0:T(8,128)S(1)}, f32[9,32,256]{2,1,0:T(8,128)S(1)}, u32[]{:S(2)}, u32[]{:S(2)}) collective-permute-start(f32[9,32,256]{2,1,0:T(8,128)S(1)} %get-tuple-element.31), channel_id=1, source_target_pairs={{0,32},{8,40},{16,184},{64,96},{72,104},{80,248},{128,160},{136,16... | collective-permute-start | bytes 884744 | tf_op jit(solution)/shard_map/ppermute | solution.py:425
  45.8 12.2 %collective-permute-start.6 = (f32[9,32,256]{2,1,0:T(8,128)S(1)}, f32[9,32,256]{2,1,0:T(8,128)S(1)}, u32[]{:S(2)}, u32[]{:S(2)}) collective-permute-start(f32[9,32,256]{2,1,0:T(8,128)S(1)} %get-tuple-element.32), channel_id=1, source_target_pairs={{0,32},{8,40},{16,48},{64,96},{72,104},{80,112},{128,160},{136,168... | collective-permute-start | bytes 884744 | tf_op jit(solution)/shard_map/ppermute | solution.py:425
  58.7 51.8 %copy-start.2 = (f32[2,9,32,256]{3,2,1,0:T(8,128)}, f32[2,9,32,256]{3,2,1,0:T(8,128)S(1)}, u32[]{:S(2)}) copy-start(f32[2,9,32,256]{3,2,1,0:T(8,128)S(1)} %hold.1.held) | copy-start | bytes 1769476
  58.7 28.5 %collective-permute-start.10 = (f32[2,9,32,256]{3,2,1,0:T(8,128)S(1)}, f32[2,9,32,256]{3,2,1,0:T(8,128)S(1)}, u32[]{:S(2)}, u32[]{:S(2)}) collective-permute-start(f32[2,9,32,256]{3,2,1,0:T(8,128)S(1)} %hold.1.held), channel_id=1, source_target_pairs={{0,16},{8,56},{16,32},{32,48},{40,24},{48,0},{56,40},{64,80},{72,1... | collective-permute-start | bytes 1769480 | tf_op jit(solution)/shard_map/ppermute | solution.py:425
  69.9 33.7 %collective-permute-start.9 = (f32[2,9,32,256]{3,2,1,0:T(8,128)S(1)}, f32[2,9,32,256]{3,2,1,0:T(8,128)S(1)}, u32[]{:S(2)}, u32[]{:S(2)}) collective-permute-start(f32[2,9,32,256]{3,2,1,0:T(8,128)S(1)} %hold.1.held), channel_id=1, source_target_pairs={{0,184},{8,128},{16,136},{32,152},{40,160},{48,168},{56,176},{64,2... | collective-permute-start | bytes 1769480 | tf_op jit(solution)/shard_map/ppermute | solution.py:425
  79.1 31.4 %collective-permute-start.8 = (f32[2,9,32,256]{3,2,1,0:T(8,128)S(1)}, f32[2,9,32,256]{3,2,1,0:T(8,128)}, u32[]{:S(2)}, u32[]{:S(2)}) collective-permute-start(f32[2,9,32,256]{3,2,1,0:T(8,128)S(1)} %hold.1.held), channel_id=1, source_target_pairs={{0,136},{8,144},{16,152},{32,168},{40,176},{48,184},{56,128},{64,2... | collective-permute-start | bytes 1769480 | tf_op jit(solution)/shard_map/ppermute | solution.py:425
  87.2 23.3 %copy-start.12 = (f32[2,9,32,256]{3,2,1,0:T(8,128)}, f32[2,9,32,256]{3,2,1,0:T(8,128)S(1)}, u32[]{:S(2)}) copy-start(f32[2,9,32,256]{3,2,1,0:T(8,128)S(1)} %collective-permute-done.10.two) | copy-start | bytes 1769476
  103.6 6.9 %copy-start.13 = (f32[2,9,32,256]{3,2,1,0:T(8,128)}, f32[2,9,32,256]{3,2,1,0:T(8,128)S(1)}, u32[]{:S(2)}) copy-start(f32[2,9,32,256]{3,2,1,0:T(8,128)S(1)} %collective-permute-done.9.before) | copy-start | bytes 1769476
  114.1 37.2 %collective-permute-start.13 = (f32[2,3,8,32,256]{4,3,2,1,0:T(8,128)}, f32[2,3,8,32,256]{4,3,2,1,0:T(8,128)}, u32[]{:S(2)}, u32[]{:S(2)}) collective-permute-start(f32[2,3,8,32,256]{4,3,2,1,0:T(8,128)} %get-tuple-element.23.after_ref.mine), channel_id=1, source_target_pairs={{0,8},{8,16},{16,24},{24,32},{32,40},{40,48},{48,56},{56,0},{64,72... | collective-permute-start | bytes 4718600 | tf_op jit(solution)/shard_map/ppermute | solution.py:425
  114.2 37.1 %collective-permute-start.12 = (f32[2,3,8,32,256]{4,3,2,1,0:T(8,128)}, f32[2,3,8,32,256]{4,3,2,1,0:T(8,128)}, u32[]{:S(2)}, u32[]{:S(2)}) collective-permute-start(f32[2,3,8,32,256]{4,3,2,1,0:T(8,128)} %get-tuple-element.23.after_ref.mine), channel_id=1, source_target_pairs={{0,192},{8,200},{16,208},{24,216},{32,224},{40,232},{48,240},{56,2... | collective-permute-start | bytes 4718600 | tf_op jit(solution)/shard_map/ppermute | solution.py:425
  114.3 37.0 %collective-permute-start.11 = (f32[2,3,8,32,256]{4,3,2,1,0:T(8,128)}, f32[2,3,8,32,256]{4,3,2,1,0:T(8,128)}, u32[]{:S(2)}, u32[]{:S(2)}) collective-permute-start(f32[2,3,8,32,256]{4,3,2,1,0:T(8,128)} %get-tuple-element.23.after_ref.mine), channel_id=1, source_target_pairs={{0,64},{8,72},{16,80},{24,88},{32,96},{40,104},{48,112},{56,120},{... | collective-permute-start | bytes 4718600 | tf_op jit(solution)/shard_map/ppermute | solution.py:425
  115.7 26.3 %all-to-all-start.2 = ((f32[8,3,2,32,256]{4,3,2,1,0:T(8,128)}), f32[8,3,2,32,256]{4,3,2,1,0:T(8,128)}, u32[]{:S(2)}, u32[]{:S(2)}) async-start(f32[8,3,2,32,256]{4,3,2,1,0:T(8,128)} %get-tuple-element.26), calls=%async_computation.2 | async-start | bytes 3145728 | tf_op jit(solution)/shard_map/all_to_all | solution.py:468
  144.3 7.1 %copy-start.4 = (f32[8,256,256]{2,1,0:T(8,128)S(1)}, f32[8,256,256]{2,1,0:T(8,128)}, u32[]{:S(2)}) copy-start(f32[8,256,256]{2,1,0:T(8,128)} %copy-done.3) | copy-start | bytes 6291460
  144.3 7.1 %copy-start.6 = (f32[8,256,256]{2,1,0:T(8,128)S(1)}, f32[8,256,256]{2,1,0:T(8,128)}, u32[]{:S(2)}) copy-start(f32[8,256,256]{2,1,0:T(8,128)} %copy-done.5) | copy-start | bytes 6291460
  (8 other events, 23.4 us)
